TPU v7x, 256 devices: a whole 4x4x8 slice. The times are simulated.
256 devices in a mesh: seq: 64 (over z, x, core), rate: 4 (over y).
Axes of the slice: x: 4, y: 4, z: 8, core: 2. Of those that a mesh axis runs over, the one named last changes fastest.
Arguments:
- projections: bfloat16 [8192, 3, 1536], P('seq'), may hold values from -10 to 10
- dilation_bits: int32 [4], P('rate'), may hold values from 0 to 3, as said below
- grad_out: bfloat16 [8192, 1536], P('seq'), may hold values from -6 to 6
Outputs:
- attended: bfloat16 [8192, 1536], P('seq', 'rate')
- grad_projections: bfloat16 [8192, 3, 1536], P('seq', None, 'rate')
Inputs may be any that keep to these rules, and one draw needn't show every extreme that they name: `dilation_bits`: each entry is a whole number from 0 to 3; some branch has 3.
All inputs are finite; a program needn't handle non-finite values.
Results may differ from a plain program's by a relative error of at most 0.014.
Values may be sent and summed in bfloat16 or wider, within the bound.
No kernel may reach another device: no remote copies, remote signals or barrier semaphores. Data moves between devices by JAX's collectives and lax.ppermute only.
A program may use at most 128 MiB of HBM per device.

v0:
```python
import jax
import jax.numpy as jnp
from jax import lax
from jax.experimental import pallas as pl
from jax.experimental.pallas import tpu as pltpu
from jax.sharding import PartitionSpec as P

HEADS = 16
HEAD_DIM = 96
TOK = 128
CHIPS = 4
OWN = HEAD_DIM * HEADS // 4
TAIL = 128 - HEAD_DIM
SEG = 8 * TOK
HALF = 4 * TOK
NEG = -1e30
LOG2E = 1.4426950408889634
SCALE = HEAD_DIM ** -0.5
BF = jnp.bfloat16
F32 = jnp.float32
RATE_ON = ((0, 1, 0, 3), (0, 2, 0, 0))
BLOCK = 3 * TOK
NOTE = 16
WIDE = 256
VMEM_LIMIT = 48 * 1024 * 1024
PREP_LIMIT = 107 * 512 * 1024


def tiles(first, second, third, spread):
    parts = []
    for t, block in enumerate((first, second, third)):
        parts.append(jnp.concatenate([block, spread[:, t * TAIL : (t + 1) * TAIL]], axis=1))
    return jnp.concatenate(parts, axis=0)


def prep_kernel(bits, proj, cot, *rest):
    outs = rest[:CHIPS]
    proj_in, cot_in, sems = rest[CHIPS:]
    chip = chip_index()
    core = lax.axis_index("seq") & 1
    copies = []
    for d in range(CHIPS):
        head = lax.rem(chip + d, CHIPS)
        on = jnp.where(core == 0, RATE_ON[0][d], RATE_ON[1][d])
        rate = lax.rem(lax.axis_index("rate") + on, CHIPS)
        cols = pl.ds(pl.multiple_of(rate * OWN + (head // 2) * TOK, TOK), 2 * TOK)
        copies.append(
            [
                pltpu.make_async_copy(proj.at[:, :, cols], proj_in.at[d], sems.at[d, 0]),
                pltpu.make_async_copy(cot.at[:, cols], cot_in.at[d], sems.at[d, 1]),
            ]
        )
    for pair in copies:
        for copy in pair:
            copy.start()
    for pair in copies:
        for copy in pair:
            copy.wait()
    rate_row = jnp.full((NOTE, TOK), bits[0].astype(F32), F32).astype(BF)
    for d in range(CHIPS):
        outs[d][BLOCK:] = rate_row
    for at in range(CHIPS):

        @pl.when(chip == at)
        def _():
            for d in range(CHIPS):
                first = ((at + d) % CHIPS * HEAD_DIM, ((at + d) % CHIPS) // 2 * TOK)
                cols = slice(first[0] - first[1], first[0] - first[1] + HEAD_DIM)
                outs[d][:BLOCK] = tiles(
                    proj_in[d, 0, :, cols], proj_in[d, 1, :, cols], proj_in[d, 2, :, cols], cot_in[d, :, cols]
                )


def chip_index():
    return lax.rem(lax.axis_index("seq") // 2, CHIPS)


def prep(bits, proj, cot):
    hbm = pl.BlockSpec(memory_space=pltpu.HBM)
    return pl.pallas_call(
        prep_kernel,
        out_shape=[jax.ShapeDtypeStruct((BLOCK + NOTE, TOK), BF)] * CHIPS,
        in_specs=[pl.BlockSpec(memory_space=pltpu.SMEM), hbm, hbm],
        out_specs=[pl.BlockSpec(memory_space=pltpu.VMEM)] * CHIPS,
        scratch_shapes=[
            pltpu.VMEM((CHIPS, 3, TOK, 2 * TOK), BF),
            pltpu.VMEM((CHIPS, TOK, 2 * TOK), BF),
            pltpu.SemaphoreType.DMA((CHIPS, 2)),
        ],
        compiler_params=pltpu.CompilerParams(vmem_limit_bytes=PREP_LIMIT),
        name="prep",
    )(bits, proj, cot)


def main_kernel(*rest):
    ins = rest[:8]
    outs = rest[8:12]
    qs, ks, vs, ds, bias, st, dp, pt, gt = rest[12:]
    chip = chip_index()
    core = lax.axis_index("seq") & 1
    lane = lax.broadcasted_iota(jnp.int32, (TOK, TOK), 1)
    for s in range(8):
        rows = pl.ds(s * TOK, TOK)
        block = ins[s]
        qs[rows] = block[:TOK]
        ks[rows] = jnp.where(lane < HEAD_DIM, block[TOK : 2 * TOK], jnp.zeros((), BF))
        vs[rows] = block[2 * TOK : BLOCK]
        ds[rows] = jnp.concatenate(
            [block[t * TOK : (t + 1) * TOK, HEAD_DIM:] for t in range(3)] + [jnp.zeros((TOK, TAIL), BF)], axis=1
        )
    key = lax.broadcasted_iota(jnp.int32, (8, TOK), 0)
    query = lax.broadcasted_iota(jnp.int32, (8, TOK), 1) & 7
    apart = key ^ query
    count = jnp.zeros((8, TOK), F32)
    noted = [ins[0][BLOCK:].astype(F32)[:8]]
    for first, second in ((1, 5), (3, 7), (5, 1)):
        noted.append(jnp.where(core == 0, ins[first][BLOCK:].astype(F32)[:8], ins[second][BLOCK:].astype(F32)[:8]))
    for level, mask in ((0, 7), (1, 3), (2, 1), (3, 0)):
        rate_bits = 3 - level
        branches = jnp.zeros((8, TOK), F32)
        for b in range(4):
            branches = branches + jnp.where(noted[b] == float(rate_bits), 1.0, 0.0)
        count = count + jnp.where((apart & mask) == 0, branches, 0.0)
        bias[level] = jnp.where(count > 0.0, jnp.log2(jnp.maximum(count, 1.0)), NEG)

    odd = chip & 1
    nt = (((1,), (1,)), ((), ()))
    for c in range(SEG // WIDE):
        cols = slice(c * WIDE, (c + 1) * WIDE)
        st[...] = lax.dot_general(ks[...], qs[cols], nt, preferred_element_type=F32)
        dp[...] = lax.dot_general(vs[...], ds[cols], nt, preferred_element_type=F32)
        for i in range(c * WIDE // TOK, (c + 1) * WIDE // TOK):
            spot = slice(i * TOK - c * WIDE, (i + 1) * TOK - c * WIDE)
            cols = slice(i * TOK, (i + 1) * TOK)
            top = None
            di = i % 4
            for j in range(8):
                dj = j % 4
                if i == j:
                    level = 3
                elif di == dj:
                    level = 2
                elif dj == (3, 2, 1, 0)[di]:
                    level = 1 - odd
                elif dj == (1, 0, 3, 2)[di]:
                    level = odd
                else:
                    level = 0
                rows = slice(j * TOK, (j + 1) * TOK)
                t = st[rows, spot].reshape(16, 8, TOK) * (SCALE * LOG2E) + bias[level][None]
                st[rows, spot] = t.reshape(TOK, TOK)
                t_top = jnp.max(t, axis=0)
                top = t_top if top is None else jnp.maximum(top, t_top)
            top = jnp.max(top, axis=0, keepdims=True)
            total = jnp.zeros((8, TOK), F32)
            inner = jnp.zeros((8, TOK), F32)
            for j in range(8):
                rows = slice(j * TOK, (j + 1) * TOK)
                e = jnp.exp2(st[rows, spot] - top)
                st[rows, spot] = e
                e3 = e.reshape(16, 8, TOK)
                total = total + jnp.sum(e3, axis=0)
                inner = inner + jnp.sum(e3 * dp[rows, spot].reshape(16, 8, TOK), axis=0)
            over = 1.0 / jnp.sum(total, axis=0, keepdims=True)
            inner = jnp.sum(inner, axis=0, keepdims=True) * over
            for j in range(8):
                if i >= 4 and j >= 4:
                    continue
                rows = slice(j * TOK, (j + 1) * TOK)
                p = st[rows, spot] * over
                pt[rows, cols] = p.astype(BF)
                gt[rows, cols] = (p * (dp[rows, spot] - inner)).astype(BF)
    nn = (((1,), (0,)), ((), ()))
    tn = (((0,), (0,)), ((), ()))
    out = jnp.transpose(lax.dot_general(vs[...], pt[:, :HALF], tn, preferred_element_type=F32))
    gq = jnp.transpose(lax.dot_general(ks[...], gt[:, :HALF], tn, preferred_element_type=F32) * SCALE)
    gv = lax.dot_general(pt[:HALF], ds[...], nn, preferred_element_type=F32)
    gk = lax.dot_general(gt[:HALF], qs[...], nn, preferred_element_type=F32) * SCALE
    for d in range(4):
        rows = slice(d * TOK, (d + 1) * TOK)
        outs[d][...] = tiles(
            out[rows, :HEAD_DIM].astype(BF), gq[rows, :HEAD_DIM].astype(BF), gk[rows, :HEAD_DIM].astype(BF), gv[rows].astype(BF)
        )


def attend(blocks):
    vmem = pl.BlockSpec(memory_space=pltpu.VMEM)
    return pl.pallas_call(
        main_kernel,
        out_shape=[jax.ShapeDtypeStruct((BLOCK, TOK), BF)] * CHIPS,
        in_specs=[vmem] * 8,
        out_specs=[vmem] * CHIPS,
        scratch_shapes=[pltpu.VMEM((SEG, TOK), BF)] * 4
        + [
            pltpu.VMEM((4, 8, TOK), F32),
            pltpu.VMEM((SEG, WIDE), F32),
            pltpu.VMEM((SEG, WIDE), F32),
            pltpu.VMEM((SEG, SEG), BF),
            pltpu.VMEM((SEG, SEG), BF),
        ],
        compiler_params=pltpu.CompilerParams(vmem_limit_bytes=VMEM_LIMIT),
        name="attend",
    )(*blocks)


def final_kernel(*rest):
    ins = rest[:4]
    attended, grads, held = rest[4:]
    chip = chip_index()
    for d in range(CHIPS):
        held[lax.rem(chip + d, CHIPS)] = ins[d][...]
    for t in range(3):
        whole = jnp.concatenate([held[h, t * TOK : (t + 1) * TOK, :HEAD_DIM] for h in range(CHIPS)], axis=1)
        if t == 0:
            attended[...] = whole
        else:
            grads[t - 1] = whole
    grads[2] = jnp.concatenate(
        [held[h, t * TOK : (t + 1) * TOK, HEAD_DIM:] for h in range(CHIPS) for t in range(3)], axis=1
    )


def final(blocks):
    vmem = pl.BlockSpec(memory_space=pltpu.VMEM)
    return pl.pallas_call(
        final_kernel,
        out_shape=[jax.ShapeDtypeStruct((TOK, OWN), BF), jax.ShapeDtypeStruct((3, TOK, OWN), BF)],
        in_specs=[vmem] * 4,
        out_specs=[vmem] * 2,
        scratch_shapes=[pltpu.VMEM((CHIPS, BLOCK, TOK), BF)],
        compiler_params=pltpu.CompilerParams(vmem_limit_bytes=VMEM_LIMIT),
        name="final",
    )(*blocks)


def moved(block, chips, flip, rates):
    seq, ring = lax.axis_size("seq"), lax.axis_size("rate")
    pairs = []
    for i in range(seq):
        to = i - i % 8 + ((i // 2 + chips) % CHIPS) * 2 + (i % 2 ^ flip)
        for r in range(ring):
            pairs.append((i * ring + r, to * ring + (r + rates[i % 2]) % ring))
    return lax.ppermute(block, ("seq", "rate"), pairs)


def body(projections, dilation_bits, grad_out):
    sent = prep(dilation_bits, jnp.transpose(projections, (1, 0, 2)), grad_out)
    near = [sent[0]] + [moved(sent[d], d, 0, (RATE_ON[0][d], RATE_ON[1][d])) for d in range(1, CHIPS)]
    far = [moved(block, 0, 1, (0, 0)) for block in near]
    results = attend(near + far)
    back = [results[0]] + [moved(results[d], -d, 0, (0, 0)) for d in range(1, CHIPS)]
    attended, grads = final(back)
    return attended, jnp.transpose(grads, (1, 0, 2))


def solution(mesh):
    in_specs = (P("seq", None, None), P("rate"), P("seq", None))
    out_specs = (P("seq", "rate"), P("seq", None, "rate"))
    return jax.shard_map(body, mesh=mesh, in_specs=in_specs, out_specs=out_specs, check_vma=False)
```

profile of v0, /device:TPU:1, one launch (start us, length us, event | category | flops | bytes accessed | tf_op | source)
XLA Modules:
  0.0 32.4 jit_solution(4076006257239779126)
XLA Ops:
  1.3 1.7 %prep.1 = (bf16[400,128]{1,0:T(8,128)(2,1)S(1)}, bf16[400,128]{1,0:T(8,128)(2,1)S(1)}, bf16[400,128]{1,0:T(8,128)(2,1)S(1)}, bf16[400,128]{1,0:T(8,128)(2,1)S(1)}) custom-call(s32[1]{0:T(128)S(6)} %copy.5.bits, bf16[3,128,1536]{2,1,0:T(8,128)(2,1)} %bitcast.2, bf16[128,1536]{1,0:T(8,128)(2,1)} %cot.1), custom_call_target="tpu_custom_call" | custom-call | tf_op jit(solution)/shard_map/prep/pallas_call | solution.py:80
  3.0 4.7 %collective-permute-start = (bf16[400,128]{1,0:T(8,128)(2,1)S(1)}, bf16[400,128]{1,0:T(8,128)(2,1)S(1)}, u32[]{:S(2)}, u32[]{:S(2)}) collective-permute-start(bf16[400,128]{1,0:T(8,128)(2,1)S(1)} %get-tuple-element.13), channel_id=1, source_target_pairs={{0,9},{1,10},{2,11},{3,8},{4,14},{5,15},{6,12},{7,13},{8,17},{9,18... | collective-permute-start | bytes 307208 | tf_op jit(solution)/shard_map/ppermute | solution.py:243
  7.7 2.4 %collective-permute-start.1 = (bf16[400,128]{1,0:T(8,128)(2,1)S(1)}, bf16[400,128]{1,0:T(8,128)(2,1)S(1)}, u32[]{:S(2)}, u32[]{:S(2)}) collective-permute-start(bf16[400,128]{1,0:T(8,128)(2,1)S(1)} %get-tuple-element.14), channel_id=1, source_target_pairs={{0,16},{1,17},{2,18},{3,19},{4,20},{5,21},{6,22},{7,23},{8,24},{9,... | collective-permute-start | bytes 307208 | tf_op jit(solution)/shard_map/ppermute | solution.py:243
  10.1 1.2 %collective-permute-start.2 = (bf16[400,128]{1,0:T(8,128)(2,1)S(1)}, bf16[400,128]{1,0:T(8,128)(2,1)S(1)}, u32[]{:S(2)}, u32[]{:S(2)}) collective-permute-start(bf16[400,128]{1,0:T(8,128)(2,1)S(1)} %get-tuple-element.15), channel_id=1, source_target_pairs={{0,27},{1,24},{2,25},{3,26},{4,28},{5,29},{6,30},{7,31},{8,3},{9,0... | collective-permute-start | bytes 307208 | tf_op jit(solution)/shard_map/ppermute | solution.py:243
  11.3 1.0 %collective-permute-start.3 = (bf16[400,128]{1,0:T(8,128)(2,1)S(1)}, bf16[400,128]{1,0:T(8,128)(2,1)S(1)}, u32[]{:S(2)}, u32[]{:S(2)}) collective-permute-start(bf16[400,128]{1,0:T(8,128)(2,1)S(1)} %get-tuple-element.12.rest_0_), channel_id=1, source_target_pairs={{0,4},{1,5},{2,6},{3,7},{4,0},{5,1},{6,2},{7,3},{8,12},{9,13},{10,... | collective-permute-start | bytes 307208 | tf_op jit(solution)/shard_map/ppermute | solution.py:243
  12.3 0.0 collective-permute-done.rest_1_
  12.3 2.0 %collective-permute-start.4 = (bf16[400,128]{1,0:T(8,128)(2,1)S(1)}, bf16[400,128]{1,0:T(8,128)(2,1)S(1)}, u32[]{:S(2)}, u32[]{:S(2)}) collective-permute-start(bf16[400,128]{1,0:T(8,128)(2,1)S(1)} %collective-permute-done.rest_1_), channel_id=1, source_target_pairs={{0,4},{1,5},{2,6},{3,7},{4,0},{5,1},{6,2},{7,3},{8,12},{9,13},{10,... | collective-permute-start | bytes 307208 | tf_op jit(solution)/shard_map/ppermute | solution.py:243
  14.3 0.7 %collective-permute-done.1.rest_2_ = bf16[400,128]{1,0:T(8,128)(2,1)S(1)} collective-permute-done((bf16[400,128]{1,0:T(8,128)(2,1)S(1)}, bf16[400,128]{1,0:T(8,128)(2,1)S(1)}, u32[]{:S(2)}, u32[]{:S(2)}) %collective-permute-start.1) | collective-permute-done | bytes 102432 | tf_op jit(solution)/shard_map/ppermute | solution.py:243
  15.0 0.3 collective-permute-start.5
  15.3 0.0 collective-permute-done.2.rest_3_
  15.3 0.6 %collective-permute-start.6 = (bf16[400,128]{1,0:T(8,128)(2,1)S(1)}, bf16[400,128]{1,0:T(8,128)(2,1)S(1)}, u32[]{:S(2)}, u32[]{:S(2)}) collective-permute-start(bf16[400,128]{1,0:T(8,128)(2,1)S(1)} %collective-permute-done.2.rest_3_), channel_id=1, source_target_pairs={{0,4},{1,5},{2,6},{3,7},{4,0},{5,1},{6,2},{7,3},{8,12},{9,13},{10,... | collective-permute-start | bytes 307208 | tf_op jit(solution)/shard_map/ppermute | solution.py:243
  15.9 0.0 collective-permute-done.3.rest_4_
  15.9 0.0 collective-permute-done.4.rest_5_
  15.9 0.4 %collective-permute-done.5.rest_6_ = bf16[400,128]{1,0:T(8,128)(2,1)S(1)} collective-permute-done((bf16[400,128]{1,0:T(8,128)(2,1)S(1)}, bf16[400,128]{1,0:T(8,128)(2,1)S(1)}, u32[]{:S(2)}, u32[]{:S(2)}) %collective-permute-start.5) | collective-permute-done | bytes 102432 | tf_op jit(solution)/shard_map/ppermute | solution.py:243
  16.3 0.5 %collective-permute-done.6.rest_7_ = bf16[400,128]{1,0:T(8,128)(2,1)S(1)} collective-permute-done((bf16[400,128]{1,0:T(8,128)(2,1)S(1)}, bf16[400,128]{1,0:T(8,128)(2,1)S(1)}, u32[]{:S(2)}, u32[]{:S(2)}) %collective-permute-start.6) | collective-permute-done | bytes 102432 | tf_op jit(solution)/shard_map/ppermute | solution.py:243
  16.8 4.2 %attend.1 = (bf16[384,128]{1,0:T(8,128)(2,1)S(1)}, bf16[384,128]{1,0:T(8,128)(2,1)S(1)}, bf16[384,128]{1,0:T(8,128)(2,1)S(1)}, bf16[384,128]{1,0:T(8,128)(2,1)S(1)}) custom-call(bf16[400,128]{1,0:T(8,128)(2,1)S(1)} %get-tuple-element.12.rest_0_, bf16[400,128]{1,0:T(8,128)(2,1)S(1)} %collective-permute-done.rest_1_, ...), custom_call_target="tpu_custom_call" | custom-call | tf_op jit(solution)/shard_map/attend/pallas_call | solution.py:188
  21.0 2.5 %collective-permute-start.7 = (bf16[384,128]{1,0:T(8,128)(2,1)S(1)}, bf16[384,128]{1,0:T(8,128)(2,1)S(1)}, u32[]{:S(2)}, u32[]{:S(2)}) collective-permute-start(bf16[384,128]{1,0:T(8,128)(2,1)S(1)} %get-tuple-element.17), channel_id=1, source_target_pairs={{0,24},{1,25},{2,26},{3,27},{4,28},{5,29},{6,30},{7,31},{8,0},{9,1... | collective-permute-start | bytes 294920 | tf_op jit(solution)/shard_map/ppermute | solution.py:243
  23.5 0.9 %collective-permute-start.8 = (bf16[384,128]{1,0:T(8,128)(2,1)S(1)}, bf16[384,128]{1,0:T(8,128)(2,1)S(1)}, u32[]{:S(2)}, u32[]{:S(2)}) collective-permute-start(bf16[384,128]{1,0:T(8,128)(2,1)S(1)} %get-tuple-element.18), channel_id=1, source_target_pairs={{0,16},{1,17},{2,18},{3,19},{4,20},{5,21},{6,22},{7,23},{8,24},{9,... | collective-permute-start | bytes 294920 | tf_op jit(solution)/shard_map/ppermute | solution.py:243
  24.3 0.4 %collective-permute-start.9 = (bf16[384,128]{1,0:T(8,128)(2,1)S(1)}, bf16[384,128]{1,0:T(8,128)(2,1)S(1)}, u32[]{:S(2)}, u32[]{:S(2)}) collective-permute-start(bf16[384,128]{1,0:T(8,128)(2,1)S(1)} %get-tuple-element.19), channel_id=1, source_target_pairs={{0,8},{1,9},{2,10},{3,11},{4,12},{5,13},{6,14},{7,15},{8,16},{9,17... | collective-permute-start | bytes 294920 | tf_op jit(solution)/shard_map/ppermute | solution.py:243
  24.7 0.4 %collective-permute-done.7.rest_1_ = bf16[384,128]{1,0:T(8,128)(2,1)S(1)} collective-permute-done((bf16[384,128]{1,0:T(8,128)(2,1)S(1)}, bf16[384,128]{1,0:T(8,128)(2,1)S(1)}, u32[]{:S(2)}, u32[]{:S(2)}) %collective-permute-start.7) | collective-permute-done | bytes 98336 | tf_op jit(solution)/shard_map/ppermute | solution.py:243
  25.2 3.3 %collective-permute-done.8.rest_2_ = bf16[384,128]{1,0:T(8,128)(2,1)S(1)} collective-permute-done((bf16[384,128]{1,0:T(8,128)(2,1)S(1)}, bf16[384,128]{1,0:T(8,128)(2,1)S(1)}, u32[]{:S(2)}, u32[]{:S(2)}) %collective-permute-start.8) | collective-permute-done | bytes 98336 | tf_op jit(solution)/shard_map/ppermute | solution.py:243
  28.5 2.9 %collective-permute-done.9.rest_3_ = bf16[384,128]{1,0:T(8,128)(2,1)S(1)} collective-permute-done((bf16[384,128]{1,0:T(8,128)(2,1)S(1)}, bf16[384,128]{1,0:T(8,128)(2,1)S(1)}, u32[]{:S(2)}, u32[]{:S(2)}) %collective-permute-start.9) | collective-permute-done | bytes 98336 | tf_op jit(solution)/shard_map/ppermute | solution.py:243
  31.4 1.0 %final.1 = (bf16[128,384]{1,0:T(8,128)(2,1)}, bf16[3,128,384]{2,1,0:T(8,128)(2,1)}) custom-call(bf16[384,128]{1,0:T(8,128)(2,1)S(1)} %get-tuple-element.16.rest_0_, bf16[384,128]{1,0:T(8,128)(2,1)S(1)} %collective-permute-done.7.rest_1_, bf16[384,128]{1,0:T(8,128)(2,1)S(1)} %collective-permute-done.8.rest_2_, bf16[384,128]{1,0:T(8,128)(2,1)S(1)} %collective-permute-done.9.rest_3_), custom_call_target="tpu_custom_call" | custom-call | tf_op jit(solution)/shard_map/final/pallas_call | solution.py:225
Async XLA Ops:
  3.0 9.3 %collective-permute-start = (bf16[400,128]{1,0:T(8,128)(2,1)S(1)}, bf16[400,128]{1,0:T(8,128)(2,1)S(1)}, u32[]{:S(2)}, u32[]{:S(2)}) collective-permute-start(bf16[400,128]{1,0:T(8,128)(2,1)S(1)} %get-tuple-element.13), channel_id=1, source_target_pairs={{0,9},{1,10},{2,11},{3,8},{4,14},{5,15},{6,12},{7,13},{8,17},{9,18... | collective-permute-start | bytes 307208 | tf_op jit(solution)/shard_map/ppermute | solution.py:243
  7.7 7.3 %collective-permute-start.1 = (bf16[400,128]{1,0:T(8,128)(2,1)S(1)}, bf16[400,128]{1,0:T(8,128)(2,1)S(1)}, u32[]{:S(2)}, u32[]{:S(2)}) collective-permute-start(bf16[400,128]{1,0:T(8,128)(2,1)S(1)} %get-tuple-element.14), channel_id=1, source_target_pairs={{0,16},{1,17},{2,18},{3,19},{4,20},{5,21},{6,22},{7,23},{8,24},{9,... | collective-permute-start | bytes 307208 | tf_op jit(solution)/shard_map/ppermute | solution.py:243
  10.1 5.1 %collective-permute-start.2 = (bf16[400,128]{1,0:T(8,128)(2,1)S(1)}, bf16[400,128]{1,0:T(8,128)(2,1)S(1)}, u32[]{:S(2)}, u32[]{:S(2)}) collective-permute-start(bf16[400,128]{1,0:T(8,128)(2,1)S(1)} %get-tuple-element.15), channel_id=1, source_target_pairs={{0,27},{1,24},{2,25},{3,26},{4,28},{5,29},{6,30},{7,31},{8,3},{9,0... | collective-permute-start | bytes 307208 | tf_op jit(solution)/shard_map/ppermute | solution.py:243
  11.3 4.6 %collective-permute-start.3 = (bf16[400,128]{1,0:T(8,128)(2,1)S(1)}, bf16[400,128]{1,0:T(8,128)(2,1)S(1)}, u32[]{:S(2)}, u32[]{:S(2)}) collective-permute-start(bf16[400,128]{1,0:T(8,128)(2,1)S(1)} %get-tuple-element.12.rest_0_), channel_id=1, source_target_pairs={{0,4},{1,5},{2,6},{3,7},{4,0},{5,1},{6,2},{7,3},{8,12},{9,13},{10,... | collective-permute-start | bytes 307208 | tf_op jit(solution)/shard_map/ppermute | solution.py:243
  12.3 3.6 %collective-permute-start.4 = (bf16[400,128]{1,0:T(8,128)(2,1)S(1)}, bf16[400,128]{1,0:T(8,128)(2,1)S(1)}, u32[]{:S(2)}, u32[]{:S(2)}) collective-permute-start(bf16[400,128]{1,0:T(8,128)(2,1)S(1)} %collective-permute-done.rest_1_), channel_id=1, source_target_pairs={{0,4},{1,5},{2,6},{3,7},{4,0},{5,1},{6,2},{7,3},{8,12},{9,13},{10,... | collective-permute-start | bytes 307208 | tf_op jit(solution)/shard_map/ppermute | solution.py:243
  15.0 1.3 %collective-permute-start.5 = (bf16[400,128]{1,0:T(8,128)(2,1)S(1)}, bf16[400,128]{1,0:T(8,128)(2,1)S(1)}, u32[]{:S(2)}, u32[]{:S(2)}) collective-permute-start(bf16[400,128]{1,0:T(8,128)(2,1)S(1)} %collective-permute-done.1.rest_2_), channel_id=1, source_target_pairs={{0,4},{1,5},{2,6},{3,7},{4,0},{5,1},{6,2},{7,3},{8,12},{9,13},{10,... | collective-permute-start | bytes 307208 | tf_op jit(solution)/shard_map/ppermute | solution.py:243
  15.3 1.6 %collective-permute-start.6 = (bf16[400,128]{1,0:T(8,128)(2,1)S(1)}, bf16[400,128]{1,0:T(8,128)(2,1)S(1)}, u32[]{:S(2)}, u32[]{:S(2)}) collective-permute-start(bf16[400,128]{1,0:T(8,128)(2,1)S(1)} %collective-permute-done.2.rest_3_), channel_id=1, source_target_pairs={{0,4},{1,5},{2,6},{3,7},{4,0},{5,1},{6,2},{7,3},{8,12},{9,13},{10,... | collective-permute-start | bytes 307208 | tf_op jit(solution)/shard_map/ppermute | solution.py:243
  21.0 4.2 %collective-permute-start.7 = (bf16[384,128]{1,0:T(8,128)(2,1)S(1)}, bf16[384,128]{1,0:T(8,128)(2,1)S(1)}, u32[]{:S(2)}, u32[]{:S(2)}) collective-permute-start(bf16[384,128]{1,0:T(8,128)(2,1)S(1)} %get-tuple-element.17), channel_id=1, source_target_pairs={{0,24},{1,25},{2,26},{3,27},{4,28},{5,29},{6,30},{7,31},{8,0},{9,1... | collective-permute-start | bytes 294920 | tf_op jit(solution)/shard_map/ppermute | solution.py:243
  23.5 5.0 %collective-permute-start.8 = (bf16[384,128]{1,0:T(8,128)(2,1)S(1)}, bf16[384,128]{1,0:T(8,128)(2,1)S(1)}, u32[]{:S(2)}, u32[]{:S(2)}) collective-permute-start(bf16[384,128]{1,0:T(8,128)(2,1)S(1)} %get-tuple-element.18), channel_id=1, source_target_pairs={{0,16},{1,17},{2,18},{3,19},{4,20},{5,21},{6,22},{7,23},{8,24},{9,... | collective-permute-start | bytes 294920 | tf_op jit(solution)/shard_map/ppermute | solution.py:243
  24.3 7.0 %collective-permute-start.9 = (bf16[384,128]{1,0:T(8,128)(2,1)S(1)}, bf16[384,128]{1,0:T(8,128)(2,1)S(1)}, u32[]{:S(2)}, u32[]{:S(2)}) collective-permute-start(bf16[384,128]{1,0:T(8,128)(2,1)S(1)} %get-tuple-element.19), channel_id=1, source_target_pairs={{0,8},{1,9},{2,10},{3,11},{4,12},{5,13},{6,14},{7,15},{8,16},{9,17... | collective-permute-start | bytes 294920 | tf_op jit(solution)/shard_map/ppermute | solution.py:243
where the time goes:
time: 32.5 us; the launch traced here: 32.4 us
  starting transfers between devices  15.9 us (49%)
  waiting for transfers between devices  8.35 us (26%)
  Pallas kernels  6.8 us (21%)
  between operations  1.3 us (4%)
    ppermute x10, starting transfers between devices, moved(): return lax.ppermute(block, ('seq', 'rate'), pairs)  15.9 us
    ppermute x10, waiting for transfers between devices, moved(): return lax.ppermute(block, ('seq', 'rate'), pairs)  8.35 us
    pallas_call x1, Pallas kernels, attend(): pl.pallas_call(main_kernel, out_shape=[jax.ShapeDtypeStruct((BLOCK, TOK),...  4.16 us
    pallas_call x1, Pallas kernels, prep(): pl.pallas_call(prep_kernel, out_shape=[jax.ShapeDtypeStruct((BLOCK + NOTE...  1.67 us
    pallas_call x1, Pallas kernels, final(): pl.pallas_call(final_kernel, out_shape=[jax.ShapeDtypeStruct((TOK, OWN),...  0.97 us
  transfers between devices with their start and end apart: 10, of which 6 were waited for; matrix products, arithmetic and copies ran while one was open for 0% of the time, Pallas kernels for 0%

commit v1 on v0

v1 whole, which is shorter than its diff:
```python
import jax
import jax.numpy as jnp
from jax import lax
from jax.experimental import pallas as pl
from jax.experimental.pallas import tpu as pltpu
from jax.sharding import PartitionSpec as P

HEADS = 16
HEAD_DIM = 96
TOK = 128
CHIPS = 4
OWN = HEAD_DIM * HEADS // 4
TAIL = 128 - HEAD_DIM
SEG = 8 * TOK
HALF = 4 * TOK
NEG = -1e30
LOG2E = 1.4426950408889634
SCALE = HEAD_DIM ** -0.5
TO_LOG2 = SCALE * LOG2E
BF = jnp.bfloat16
F32 = jnp.float32
MADE = ((0, (0, 0), True), (1, (1, 2), True), (2, (0, 0), False), (3, (0, 0), False), (0, (3, 3), True))
BLOCK = 3 * TOK
NOTE = 16
WIDE = 256
VMEM_LIMIT = 48 * 1024 * 1024
PREP_LIMIT = 213 * 256 * 1024


def tiles(first, second, third, spread):
    parts = []
    for t, block in enumerate((first, second, third)):
        parts.append(jnp.concatenate([block, spread[:, t * TAIL : (t + 1) * TAIL]], axis=1))
    return jnp.concatenate(parts, axis=0)


def prep_kernel(bits, proj, cot, *rest):
    outs = rest[: len(MADE)]
    proj_in, cot_in, sems = rest[len(MADE) :]
    chip = chip_index()
    core = lax.axis_index("seq") & 1
    copies = []
    for e, (step, on, _) in enumerate(MADE):
        head = lax.rem(chip + step, CHIPS)
        rate = lax.rem(lax.axis_index("rate") + jnp.where(core == 0, on[0], on[1]), CHIPS)
        cols = pl.ds(pl.multiple_of(rate * OWN + (head // 2) * TOK, TOK), 2 * TOK)
        copies.append(
            [
                pltpu.make_async_copy(proj.at[:, :, cols], proj_in.at[e], sems.at[e, 0]),
                pltpu.make_async_copy(cot.at[:, cols], cot_in.at[e], sems.at[e, 1]),
            ]
        )
    for pair in copies:
        for copy in pair:
            copy.start()
    note = jnp.full((NOTE, TOK), bits[0].astype(F32), F32).astype(BF)
    for e, (_, _, noted) in enumerate(MADE):
        if noted:
            outs[e][BLOCK:] = note
    for at in range(CHIPS):

        @pl.when(chip == at)
        def _():
            for e, (step, _, _) in enumerate(MADE):
                head = (at + step) % CHIPS
                first = head * HEAD_DIM - head // 2 * TOK
                cols = slice(first, first + HEAD_DIM)
                for copy in copies[e]:
                    copy.wait()
                outs[e][:BLOCK] = tiles(
                    proj_in[e, 0, :, cols], proj_in[e, 1, :, cols], proj_in[e, 2, :, cols], cot_in[e, :, cols]
                )


def chip_index():
    return lax.rem(lax.axis_index("seq") // 2, CHIPS)


def prep(bits, proj, cot):
    hbm = pl.BlockSpec(memory_space=pltpu.HBM)
    return pl.pallas_call(
        prep_kernel,
        out_shape=[jax.ShapeDtypeStruct((BLOCK + NOTE * noted, TOK), BF) for _, _, noted in MADE],
        in_specs=[pl.BlockSpec(memory_space=pltpu.SMEM), hbm, hbm],
        out_specs=[pl.BlockSpec(memory_space=pltpu.VMEM)] * len(MADE),
        scratch_shapes=[
            pltpu.VMEM((len(MADE), 3, TOK, 2 * TOK), BF),
            pltpu.VMEM((len(MADE), TOK, 2 * TOK), BF),
            pltpu.SemaphoreType.DMA((len(MADE), 2)),
        ],
        compiler_params=pltpu.CompilerParams(vmem_limit_bytes=PREP_LIMIT),
        name="prep",
    )(bits, proj, cot)


def near_level(i, j, odd):
    if i == j:
        return 3
    if i % 4 == j % 4:
        return 2
    if j % 4 == (3, 2, 1, 0)[i % 4]:
        return 1 - odd
    if j % 4 == (1, 0, 3, 2)[i % 4]:
        return odd
    return 0


def main_kernel(*rest):
    ins = rest[:8]
    outs = rest[8:12]
    qs, ks, vs, ds, bias, st, dp, et, gt, qn, dn, out, gq, gk, gv = rest[12:]
    odd = chip_index() & 1
    nn = (((1,), (0,)), ((), ()))
    nt = (((1,), (1,)), ((), ()))
    tn = (((0,), (0,)), ((), ()))
    lane = lax.broadcasted_iota(jnp.int32, (TOK, TOK), 1)
    for s in range(8):
        rows = pl.ds(s * TOK, TOK)
        block = ins[s]
        qs[rows] = block[:TOK]
        ks[rows] = jnp.where(lane < HEAD_DIM, block[TOK : 2 * TOK], jnp.zeros((), BF))
        vs[rows] = jnp.where(
            lane < HEAD_DIM, block[2 * TOK : BLOCK], jnp.where(lane == HEAD_DIM, jnp.ones((), BF), jnp.zeros((), BF))
        )
        ds[rows] = jnp.concatenate(
            [block[t * TOK : (t + 1) * TOK, HEAD_DIM:] for t in range(3)] + [jnp.zeros((TOK, TAIL), BF)], axis=1
        )
    key = lax.broadcasted_iota(jnp.int32, (8, TOK), 0)
    query = lax.broadcasted_iota(jnp.int32, (8, TOK), 1) & 7
    apart = key ^ query
    count = jnp.zeros((8, TOK), F32)
    noted = [ins[e][BLOCK:].astype(F32)[:8] for e in (0, 1, 4, 5)]
    for level, mask in ((0, 7), (1, 3), (2, 1), (3, 0)):
        rate_bits = 3 - level
        branches = jnp.zeros((8, TOK), F32)
        for b in range(4):
            branches = branches + jnp.where(noted[b] == float(rate_bits), 1.0, 0.0)
        count = count + jnp.where((apart & mask) == 0, branches, 0.0)
        bias[level] = jnp.where(count > 0.0, jnp.log2(jnp.maximum(count, 1.0)) * (1.0 / TO_LOG2), NEG)

    def products(c):
        cols = slice(c * WIDE, (c + 1) * WIDE)
        st[c] = lax.dot_general(ks[...], qs[cols], nt, preferred_element_type=F32)
        dp[c] = lax.dot_general(vs[...], ds[cols], nt, preferred_element_type=F32)

    def weights(c):
        for i in range(c * WIDE // TOK, (c + 1) * WIDE // TOK):
            spot = slice(i * TOK - c * WIDE, (i + 1) * TOK - c * WIDE)
            cols = slice(i * TOK, (i + 1) * TOK)
            near = [bias[near_level(i, j, odd)] for j in range(8)]
            top = None
            for j in range(8):
                rows = slice(j * TOK, (j + 1) * TOK)
                j_top = jnp.max(st[c, rows, spot].reshape(16, 8, TOK) + near[j][None], axis=0)
                top = j_top if top is None else jnp.maximum(top, j_top)
            top = jnp.max(top, axis=0, keepdims=True)
            for j in range(8):
                rows = slice(j * TOK, (j + 1) * TOK)
                t = st[c, rows, spot].reshape(16, 8, TOK) + (near[j] - top)[None]
                et[rows, cols] = jnp.exp2(t * TO_LOG2).reshape(TOK, TOK).astype(BF)

    def scores(c):
        cols = slice(c * WIDE, (c + 1) * WIDE)
        summed = lax.dot_general(vs[...], et[:, cols], tn, preferred_element_type=F32)
        over = 1.0 / summed[HEAD_DIM : HEAD_DIM + 1]
        merged = summed * over
        if c * WIDE < HALF:
            out[cols] = jnp.transpose(merged)
        inner = jnp.sum(merged * jnp.transpose(ds[cols].astype(F32)), axis=0, keepdims=True)
        for i in range(c * WIDE // TOK, (c + 1) * WIDE // TOK):
            spot = slice(i * TOK - c * WIDE, (i + 1) * TOK - c * WIDE)
            cols = slice(i * TOK, (i + 1) * TOK)
            for j in range(4 if i >= 4 else 8):
                rows = slice(j * TOK, (j + 1) * TOK)
                gt[rows, cols] = (et[rows, cols].astype(F32) * (dp[c, rows, spot] - inner[:, spot])).astype(BF)
            upright = jnp.transpose(jnp.broadcast_to(over[:, spot], (TOK, TOK)))
            qn[cols] = (qs[cols].astype(F32) * (upright * SCALE)).astype(BF)
            dn[cols] = (ds[cols].astype(F32) * upright).astype(BF)
        return over

    chunks = SEG // WIDE
    products(0)
    overs = []
    for c in range(chunks):
        if c + 1 < chunks:
            products(c + 1)
        weights(c)
        overs.append(scores(c))
    part = lax.dot_general(ks[...], gt[:, :HALF], tn, preferred_element_type=F32)
    gq[...] = jnp.transpose(part * (jnp.concatenate(overs[: HALF // WIDE], axis=1) * SCALE))
    gv[...] = lax.dot_general(et[:HALF], dn[...], nn, preferred_element_type=F32)
    gk[...] = lax.dot_general(gt[:HALF], qn[...], nn, preferred_element_type=F32)
    for d in range(4):
        rows = slice(d * TOK, (d + 1) * TOK)
        outs[d][...] = tiles(
            out[rows, :HEAD_DIM].astype(BF), gq[rows, :HEAD_DIM].astype(BF), gk[rows, :HEAD_DIM].astype(BF), gv[rows].astype(BF)
        )


def attend(blocks):
    vmem = pl.BlockSpec(memory_space=pltpu.VMEM)
    return pl.pallas_call(
        main_kernel,
        out_shape=[jax.ShapeDtypeStruct((BLOCK, TOK), BF)] * CHIPS,
        in_specs=[vmem] * 8,
        out_specs=[vmem] * CHIPS,
        scratch_shapes=[pltpu.VMEM((SEG, TOK), BF)] * 4
        + [
            pltpu.VMEM((4, 8, TOK), F32),
            pltpu.VMEM((SEG // WIDE, SEG, WIDE), F32),
            pltpu.VMEM((SEG // WIDE, SEG, WIDE), F32),
            pltpu.VMEM((SEG, SEG), BF),
            pltpu.VMEM((SEG, SEG), BF),
            pltpu.VMEM((SEG, TOK), BF),
            pltpu.VMEM((SEG, TOK), BF),
        ]
        + [pltpu.VMEM((HALF, TOK), F32)] * 4,
        compiler_params=pltpu.CompilerParams(vmem_limit_bytes=VMEM_LIMIT),
        name="attend",
    )(*blocks)


def final_kernel(*rest):
    ins = rest[:4]
    attended, grads, held, sems = rest[4:]
    chip = chip_index()
    copies = [pltpu.make_async_copy(held.at[0], attended, sems.at[0])]
    for t in range(3):
        copies.append(pltpu.make_async_copy(held.at[t + 1], grads.at[t], sems.at[t + 1]))
    for at in range(CHIPS):

        @pl.when(chip == at)
        def _():
            blocks = [ins[(h - at) % CHIPS] for h in range(CHIPS)]
            for t in range(3):
                held[t] = jnp.concatenate([block[t * TOK : (t + 1) * TOK, :HEAD_DIM] for block in blocks], axis=1)
                copies[t].start()
            held[3] = jnp.concatenate(
                [block[t * TOK : (t + 1) * TOK, HEAD_DIM:] for block in blocks for t in range(3)], axis=1
            )
            copies[3].start()

    for copy in copies:
        copy.wait()


def final(blocks):
    vmem = pl.BlockSpec(memory_space=pltpu.VMEM)
    hbm = pl.BlockSpec(memory_space=pltpu.HBM)
    return pl.pallas_call(
        final_kernel,
        out_shape=[jax.ShapeDtypeStruct((TOK, OWN), BF), jax.ShapeDtypeStruct((3, TOK, OWN), BF)],
        in_specs=[vmem] * 4,
        out_specs=[hbm] * 2,
        scratch_shapes=[pltpu.VMEM((4, TOK, OWN), BF), pltpu.SemaphoreType.DMA((4,))],
        compiler_params=pltpu.CompilerParams(vmem_limit_bytes=VMEM_LIMIT),
        name="final",
    )(*blocks)


def moved(block, chips, flip, rates):
    seq, ring = lax.axis_size("seq"), lax.axis_size("rate")
    pairs = []
    for i in range(seq):
        to = i - i % 8 + ((i // 2 + chips) % CHIPS) * 2 + (i % 2 ^ flip)
        for r in range(ring):
            pairs.append((i * ring + r, to * ring + (r + rates[i % 2]) % ring))
    return lax.ppermute(block, ("seq", "rate"), pairs)


def body(projections, dilation_bits, grad_out):
    sent = prep(dilation_bits, jnp.transpose(projections, (1, 0, 2)), grad_out)
    near = [sent[0]] + [moved(sent[e], MADE[e][0], 0, MADE[e][1]) for e in range(1, CHIPS)]
    far = [moved(sent[CHIPS], 0, 1, MADE[CHIPS][1])] + [moved(block, 0, 1, (0, 0)) for block in near[1:]]
    results = attend(near + far)
    back = [results[0]] + [moved(results[d], -d, 0, (0, 0)) for d in range(1, CHIPS)]
    attended, grads = final(back)
    return attended, jnp.transpose(grads, (1, 0, 2))


def solution(mesh):
    in_specs = (P("seq", None, None), P("rate"), P("seq", None))
    out_specs = (P("seq", "rate"), P("seq", None, "rate"))
    return jax.shard_map(body, mesh=mesh, in_specs=in_specs, out_specs=out_specs, check_vma=False)
```

time: 32.5 us -> 31.4 us (0.966)
  starting transfers between devices: 15.9 us -> 15.1 us
  Pallas kernels: 6.8 us -> 6.35 us
    ppermute x10, starting transfers between devices: 15.9 us -> 15.1 us  [moved(): return lax.ppermute(block, ('seq', 'rate'), pairs)]
    pallas_call x1, Pallas kernels: 4.16 us -> 3.77 us  [attend(): pl.pallas_call(main_kernel, out_shape=[jax.ShapeDtypeStruct((BLOCK, TOK),...]
  transfers between devices with their start and end apart: 10 -> 10, of which waited for: 6 -> 7; matrix products, arithmetic and copies ran while one was open for 0% -> 0% of each run, Pallas kernels for 0% -> 0%
where the time goes in v1:
time: 31.4 us; the launch traced here: 31.3 us
  starting transfers between devices  15.1 us (48%)
  waiting for transfers between devices  8.48 us (27%)
  Pallas kernels  6.35 us (20%)
  between operations  1.3 us (4%)
    ppermute x10, starting transfers between devices, moved(): return lax.ppermute(block, ('seq', 'rate'), pairs)  15.1 us
    ppermute x10, waiting for transfers between devices, moved(): return lax.ppermute(block, ('seq', 'rate'), pairs)  8.48 us
    pallas_call x1, Pallas kernels, attend(): pl.pallas_call(main_kernel, out_shape=[jax.ShapeDtypeStruct((BLOCK, TOK),...  3.77 us
    pallas_call x1, Pallas kernels, prep(): pl.pallas_call(prep_kernel, out_shape=[jax.ShapeDtypeStruct((BLOCK + NOTE...  1.68 us
    pallas_call x1, Pallas kernels, final(): pl.pallas_call(final_kernel, out_shape=[jax.ShapeDtypeStruct((TOK, OWN),...  0.9 us
  transfers between devices with their start and end apart: 10, of which 7 were waited for; matrix products, arithmetic and copies ran while one was open for 0% of the time, Pallas kernels for 0%

profile of v1, /device:TPU:1, one launch (start us, length us, event | category | flops | bytes accessed | tf_op | source)
XLA Modules:
  0.0 31.3 jit_solution(17404159988892957300)
XLA Ops:
  1.3 1.7 %prep.1 = (bf16[400,128]{1,0:T(8,128)(2,1)S(1)}, bf16[400,128]{1,0:T(8,128)(2,1)S(1)}, bf16[384,128]{1,0:T(8,128)(2,1)S(1)}, bf16[384,128]{1,0:T(8,128)(2,1)S(1)}, bf16[400,128]{1,0:T(8,128)(2,1)S(1)}) custom-call(s32[1]{0:T(128)S(6)} %copy.5.bits, bf16[3,128,1536]{2,1,0:T(8,128)(2,1)} %bitcast.2, bf16[128,1536]{1,0:T(8,128)(2,1)} %cot.1), custom_call_target="tpu_custom_call" | custom-call | tf_op jit(solution)/shard_map/prep/pallas_call | solution.py:81
  3.0 4.7 %collective-permute-start = (bf16[400,128]{1,0:T(8,128)(2,1)S(1)}, bf16[400,128]{1,0:T(8,128)(2,1)S(1)}, u32[]{:S(2)}, u32[]{:S(2)}) collective-permute-start(bf16[400,128]{1,0:T(8,128)(2,1)S(1)} %get-tuple-element.14), channel_id=1, source_target_pairs={{0,9},{1,10},{2,11},{3,8},{4,14},{5,15},{6,12},{7,13},{8,17},{9,18... | collective-permute-start | bytes 307208 | tf_op jit(solution)/shard_map/ppermute | solution.py:268
  7.7 2.5 %collective-permute-start.1 = (bf16[384,128]{1,0:T(8,128)(2,1)S(1)}, bf16[384,128]{1,0:T(8,128)(2,1)S(1)}, u32[]{:S(2)}, u32[]{:S(2)}) collective-permute-start(bf16[384,128]{1,0:T(8,128)(2,1)S(1)} %get-tuple-element.15), channel_id=1, source_target_pairs={{0,16},{1,17},{2,18},{3,19},{4,20},{5,21},{6,22},{7,23},{8,24},{9,... | collective-permute-start | bytes 294920 | tf_op jit(solution)/shard_map/ppermute | solution.py:268
  10.2 1.1 %collective-permute-start.2 = (bf16[384,128]{1,0:T(8,128)(2,1)S(1)}, bf16[384,128]{1,0:T(8,128)(2,1)S(1)}, u32[]{:S(2)}, u32[]{:S(2)}) collective-permute-start(bf16[384,128]{1,0:T(8,128)(2,1)S(1)} %get-tuple-element.16), channel_id=1, source_target_pairs={{0,24},{1,25},{2,26},{3,27},{4,28},{5,29},{6,30},{7,31},{8,0},{9,1... | collective-permute-start | bytes 294920 | tf_op jit(solution)/shard_map/ppermute | solution.py:268
  11.3 1.2 %collective-permute-start.3 = (bf16[400,128]{1,0:T(8,128)(2,1)S(1)}, bf16[400,128]{1,0:T(8,128)(2,1)S(1)}, u32[]{:S(2)}, u32[]{:S(2)}) collective-permute-start(bf16[400,128]{1,0:T(8,128)(2,1)S(1)} %get-tuple-element.17), channel_id=1, source_target_pairs={{0,7},{1,4},{2,5},{3,6},{4,3},{5,0},{6,1},{7,2},{8,15},{9,12},{10,... | collective-permute-start | bytes 307208 | tf_op jit(solution)/shard_map/ppermute | solution.py:268
  12.5 0.0 collective-permute-done.rest_1_
  12.5 1.8 %collective-permute-start.4 = (bf16[400,128]{1,0:T(8,128)(2,1)S(1)}, bf16[400,128]{1,0:T(8,128)(2,1)S(1)}, u32[]{:S(2)}, u32[]{:S(2)}) collective-permute-start(bf16[400,128]{1,0:T(8,128)(2,1)S(1)} %collective-permute-done.rest_1_), channel_id=1, source_target_pairs={{0,4},{1,5},{2,6},{3,7},{4,0},{5,1},{6,2},{7,3},{8,12},{9,13},{10,... | collective-permute-start | bytes 307208 | tf_op jit(solution)/shard_map/ppermute | solution.py:268
  14.3 0.7 %collective-permute-done.1.rest_2_ = bf16[384,128]{1,0:T(8,128)(2,1)S(1)} collective-permute-done((bf16[384,128]{1,0:T(8,128)(2,1)S(1)}, bf16[384,128]{1,0:T(8,128)(2,1)S(1)}, u32[]{:S(2)}, u32[]{:S(2)}) %collective-permute-start.1) | collective-permute-done | bytes 98336 | tf_op jit(solution)/shard_map/ppermute | solution.py:268
  15.0 0.3 collective-permute-start.5
  15.2 0.0 collective-permute-done.2.rest_3_
  15.2 0.2 collective-permute-start.6
  15.5 0.2 collective-permute-done.3.rest_4_
  15.7 0.5 %collective-permute-done.5.rest_6_ = bf16[384,128]{1,0:T(8,128)(2,1)S(1)} collective-permute-done((bf16[384,128]{1,0:T(8,128)(2,1)S(1)}, bf16[384,128]{1,0:T(8,128)(2,1)S(1)}, u32[]{:S(2)}, u32[]{:S(2)}) %collective-permute-start.5) | collective-permute-done | bytes 98336 | tf_op jit(solution)/shard_map/ppermute | solution.py:268
  16.3 0.3 collective-permute-done.6.rest_7_
  16.5 0.0 collective-permute-done.4.rest_5_
  16.5 3.8 %attend.1 = (bf16[384,128]{1,0:T(8,128)(2,1)S(1)}, bf16[384,128]{1,0:T(8,128)(2,1)S(1)}, bf16[384,128]{1,0:T(8,128)(2,1)S(1)}, bf16[384,128]{1,0:T(8,128)(2,1)S(1)}) custom-call(bf16[400,128]{1,0:T(8,128)(2,1)S(1)} %get-tuple-element.13.rest_0_, bf16[400,128]{1,0:T(8,128)(2,1)S(1)} %collective-permute-done.rest_1_, ...), custom_call_target="tpu_custom_call" | custom-call | tf_op jit(solution)/shard_map/attend/pallas_call | solution.py:202
  20.3 2.3 %collective-permute-start.7 = (bf16[384,128]{1,0:T(8,128)(2,1)S(1)}, bf16[384,128]{1,0:T(8,128)(2,1)S(1)}, u32[]{:S(2)}, u32[]{:S(2)}) collective-permute-start(bf16[384,128]{1,0:T(8,128)(2,1)S(1)} %get-tuple-element.19), channel_id=1, source_target_pairs={{0,24},{1,25},{2,26},{3,27},{4,28},{5,29},{6,30},{7,31},{8,0},{9,1... | collective-permute-start | bytes 294920 | tf_op jit(solution)/shard_map/ppermute | solution.py:268
  22.6 1.1 %collective-permute-start.8 = (bf16[384,128]{1,0:T(8,128)(2,1)S(1)}, bf16[384,128]{1,0:T(8,128)(2,1)S(1)}, u32[]{:S(2)}, u32[]{:S(2)}) collective-permute-start(bf16[384,128]{1,0:T(8,128)(2,1)S(1)} %get-tuple-element.20), channel_id=1, source_target_pairs={{0,16},{1,17},{2,18},{3,19},{4,20},{5,21},{6,22},{7,23},{8,24},{9,... | collective-permute-start | bytes 294920 | tf_op jit(solution)/shard_map/ppermute | solution.py:268
  23.6 0.0 collective-permute-start.9
  23.7 0.9 %collective-permute-done.7.rest_1_ = bf16[384,128]{1,0:T(8,128)(2,1)S(1)} collective-permute-done((bf16[384,128]{1,0:T(8,128)(2,1)S(1)}, bf16[384,128]{1,0:T(8,128)(2,1)S(1)}, u32[]{:S(2)}, u32[]{:S(2)}) %collective-permute-start.7) | collective-permute-done | bytes 98336 | tf_op jit(solution)/shard_map/ppermute | solution.py:268
  24.6 3.0 %collective-permute-done.8.rest_2_ = bf16[384,128]{1,0:T(8,128)(2,1)S(1)} collective-permute-done((bf16[384,128]{1,0:T(8,128)(2,1)S(1)}, bf16[384,128]{1,0:T(8,128)(2,1)S(1)}, u32[]{:S(2)}, u32[]{:S(2)}) %collective-permute-start.8) | collective-permute-done | bytes 98336 | tf_op jit(solution)/shard_map/ppermute | solution.py:268
  27.6 2.8 %collective-permute-done.9.rest_3_ = bf16[384,128]{1,0:T(8,128)(2,1)S(1)} collective-permute-done((bf16[384,128]{1,0:T(8,128)(2,1)S(1)}, bf16[384,128]{1,0:T(8,128)(2,1)S(1)}, u32[]{:S(2)}, u32[]{:S(2)}) %collective-permute-start.9) | collective-permute-done | bytes 98336 | tf_op jit(solution)/shard_map/ppermute | solution.py:268
  30.4 0.9 %final.1 = (bf16[128,384]{1,0:T(8,128)(2,1)}, bf16[3,128,384]{2,1,0:T(8,128)(2,1)}) custom-call(bf16[384,128]{1,0:T(8,128)(2,1)S(1)} %get-tuple-element.18.rest_0_, bf16[384,128]{1,0:T(8,128)(2,1)S(1)} %collective-permute-done.7.rest_1_, bf16[384,128]{1,0:T(8,128)(2,1)S(1)} %collective-permute-done.8.rest_2_, bf16[384,128]{1,0:T(8,128)(2,1)S(1)} %collective-permute-done.9.rest_3_), custom_call_target="tpu_custom_call" | custom-call | tf_op jit(solution)/shard_map/final/pallas_call | solution.py:250
Async XLA Ops:
  3.0 9.5 %collective-permute-start = (bf16[400,128]{1,0:T(8,128)(2,1)S(1)}, bf16[400,128]{1,0:T(8,128)(2,1)S(1)}, u32[]{:S(2)}, u32[]{:S(2)}) collective-permute-start(bf16[400,128]{1,0:T(8,128)(2,1)S(1)} %get-tuple-element.14), channel_id=1, source_target_pairs={{0,9},{1,10},{2,11},{3,8},{4,14},{5,15},{6,12},{7,13},{8,17},{9,18... | collective-permute-start | bytes 307208 | tf_op jit(solution)/shard_map/ppermute | solution.py:268
  7.7 7.2 %collective-permute-start.1 = (bf16[384,128]{1,0:T(8,128)(2,1)S(1)}, bf16[384,128]{1,0:T(8,128)(2,1)S(1)}, u32[]{:S(2)}, u32[]{:S(2)}) collective-permute-start(bf16[384,128]{1,0:T(8,128)(2,1)S(1)} %get-tuple-element.15), channel_id=1, source_target_pairs={{0,16},{1,17},{2,18},{3,19},{4,20},{5,21},{6,22},{7,23},{8,24},{9,... | collective-permute-start | bytes 294920 | tf_op jit(solution)/shard_map/ppermute | solution.py:268
  10.2 5.1 %collective-permute-start.2 = (bf16[384,128]{1,0:T(8,128)(2,1)S(1)}, bf16[384,128]{1,0:T(8,128)(2,1)S(1)}, u32[]{:S(2)}, u32[]{:S(2)}) collective-permute-start(bf16[384,128]{1,0:T(8,128)(2,1)S(1)} %get-tuple-element.16), channel_id=1, source_target_pairs={{0,24},{1,25},{2,26},{3,27},{4,28},{5,29},{6,30},{7,31},{8,0},{9,1... | collective-permute-start | bytes 294920 | tf_op jit(solution)/shard_map/ppermute | solution.py:268
  11.3 4.4 %collective-permute-start.3 = (bf16[400,128]{1,0:T(8,128)(2,1)S(1)}, bf16[400,128]{1,0:T(8,128)(2,1)S(1)}, u32[]{:S(2)}, u32[]{:S(2)}) collective-permute-start(bf16[400,128]{1,0:T(8,128)(2,1)S(1)} %get-tuple-element.17), channel_id=1, source_target_pairs={{0,7},{1,4},{2,5},{3,6},{4,3},{5,0},{6,1},{7,2},{8,15},{9,12},{10,... | collective-permute-start | bytes 307208 | tf_op jit(solution)/shard_map/ppermute | solution.py:268
  12.5 4.1 %collective-permute-start.4 = (bf16[400,128]{1,0:T(8,128)(2,1)S(1)}, bf16[400,128]{1,0:T(8,128)(2,1)S(1)}, u32[]{:S(2)}, u32[]{:S(2)}) collective-permute-start(bf16[400,128]{1,0:T(8,128)(2,1)S(1)} %collective-permute-done.rest_1_), channel_id=1, source_target_pairs={{0,4},{1,5},{2,6},{3,7},{4,0},{5,1},{6,2},{7,3},{8,12},{9,13},{10,... | collective-permute-start | bytes 307208 | tf_op jit(solution)/shard_map/ppermute | solution.py:268
  15.0 1.3 %collective-permute-start.5 = (bf16[384,128]{1,0:T(8,128)(2,1)S(1)}, bf16[384,128]{1,0:T(8,128)(2,1)S(1)}, u32[]{:S(2)}, u32[]{:S(2)}) collective-permute-start(bf16[384,128]{1,0:T(8,128)(2,1)S(1)} %collective-permute-done.1.rest_2_), channel_id=1, source_target_pairs={{0,4},{1,5},{2,6},{3,7},{4,0},{5,1},{6,2},{7,3},{8,12},{9,13},{10,... | collective-permute-start | bytes 294920 | tf_op jit(solution)/shard_map/ppermute | solution.py:268
  15.2 1.3 %collective-permute-start.6 = (bf16[384,128]{1,0:T(8,128)(2,1)S(1)}, bf16[384,128]{1,0:T(8,128)(2,1)S(1)}, u32[]{:S(2)}, u32[]{:S(2)}) collective-permute-start(bf16[384,128]{1,0:T(8,128)(2,1)S(1)} %collective-permute-done.2.rest_3_), channel_id=1, source_target_pairs={{0,4},{1,5},{2,6},{3,7},{4,0},{5,1},{6,2},{7,3},{8,12},{9,13},{10,... | collective-permute-start | bytes 294920 | tf_op jit(solution)/shard_map/ppermute | solution.py:268
  20.3 4.3 %collective-permute-start.7 = (bf16[384,128]{1,0:T(8,128)(2,1)S(1)}, bf16[384,128]{1,0:T(8,128)(2,1)S(1)}, u32[]{:S(2)}, u32[]{:S(2)}) collective-permute-start(bf16[384,128]{1,0:T(8,128)(2,1)S(1)} %get-tuple-element.19), channel_id=1, source_target_pairs={{0,24},{1,25},{2,26},{3,27},{4,28},{5,29},{6,30},{7,31},{8,0},{9,1... | collective-permute-start | bytes 294920 | tf_op jit(solution)/shard_map/ppermute | solution.py:268
  22.6 5.0 %collective-permute-start.8 = (bf16[384,128]{1,0:T(8,128)(2,1)S(1)}, bf16[384,128]{1,0:T(8,128)(2,1)S(1)}, u32[]{:S(2)}, u32[]{:S(2)}) collective-permute-start(bf16[384,128]{1,0:T(8,128)(2,1)S(1)} %get-tuple-element.20), channel_id=1, source_target_pairs={{0,16},{1,17},{2,18},{3,19},{4,20},{5,21},{6,22},{7,23},{8,24},{9,... | collective-permute-start | bytes 294920 | tf_op jit(solution)/shard_map/ppermute | solution.py:268
  23.6 6.7 %collective-permute-start.9 = (bf16[384,128]{1,0:T(8,128)(2,1)S(1)}, bf16[384,128]{1,0:T(8,128)(2,1)S(1)}, u32[]{:S(2)}, u32[]{:S(2)}) collective-permute-start(bf16[384,128]{1,0:T(8,128)(2,1)S(1)} %get-tuple-element.21), channel_id=1, source_target_pairs={{0,8},{1,9},{2,10},{3,11},{4,12},{5,13},{6,14},{7,15},{8,16},{9,17... | collective-permute-start | bytes 294920 | tf_op jit(solution)/shard_map/ppermute | solution.py:268

commit v2 on v1

--- a/solution.py
+++ b/solution.py
@@ -20,6 +20,7 @@
 BF = jnp.bfloat16
 F32 = jnp.float32
 MADE = ((0, (0, 0), True), (1, (1, 2), True), (2, (0, 0), False), (3, (0, 0), False), (0, (3, 3), True))
+BACK = (0, 2, 3, 1)
 BLOCK = 3 * TOK
 NOTE = 16
 WIDE = 256
@@ -190,11 +191,21 @@
     gq[...] = jnp.transpose(part * (jnp.concatenate(overs[: HALF // WIDE], axis=1) * SCALE))
     gv[...] = lax.dot_general(et[:HALF], dn[...], nn, preferred_element_type=F32)
     gk[...] = lax.dot_general(gt[:HALF], qn[...], nn, preferred_element_type=F32)
+    made = []
     for d in range(4):
         rows = slice(d * TOK, (d + 1) * TOK)
-        outs[d][...] = tiles(
-            out[rows, :HEAD_DIM].astype(BF), gq[rows, :HEAD_DIM].astype(BF), gk[rows, :HEAD_DIM].astype(BF), gv[rows].astype(BF)
-        )
+        made.append(
+            tiles(
+                out[rows, :HEAD_DIM].astype(BF),
+                gq[rows, :HEAD_DIM].astype(BF),
+                gk[rows, :HEAD_DIM].astype(BF),
+                gv[rows].astype(BF),
+            )
+        )
+    outs[0][...] = made[0]
+    outs[1][...] = jnp.where(odd == 1, made[1], made[3])
+    outs[2][...] = made[2]
+    outs[3][...] = jnp.where(odd == 1, made[3], made[1])
 
 
 def attend(blocks):
@@ -231,7 +242,7 @@
 
         @pl.when(chip == at)
         def _():
-            blocks = [ins[(h - at) % CHIPS] for h in range(CHIPS)]
+            blocks = [ins[BACK.index(h ^ at)] for h in range(CHIPS)]
             for t in range(3):
                 held[t] = jnp.concatenate([block[t * TOK : (t + 1) * TOK, :HEAD_DIM] for block in blocks], axis=1)
                 copies[t].start()
@@ -268,12 +279,16 @@
     return lax.ppermute(block, ("seq", "rate"), pairs)
 
 
+def traded(block, across):
+    return lax.ppermute(block, "seq", [(i, i ^ across * 2) for i in range(lax.axis_size("seq"))])
+
+
 def body(projections, dilation_bits, grad_out):
     sent = prep(dilation_bits, jnp.transpose(projections, (1, 0, 2)), grad_out)
     near = [sent[0]] + [moved(sent[e], MADE[e][0], 0, MADE[e][1]) for e in range(1, CHIPS)]
     far = [moved(sent[CHIPS], 0, 1, MADE[CHIPS][1])] + [moved(block, 0, 1, (0, 0)) for block in near[1:]]
     results = attend(near + far)
-    back = [results[0]] + [moved(results[d], -d, 0, (0, 0)) for d in range(1, CHIPS)]
+    back = [traded(results[k], k) if k else results[k] for k in BACK]
     attended, grads = final(back)
     return attended, jnp.transpose(grads, (1, 0, 2))
 

time: 31.4 us -> 29.3 us (0.933)
  waiting for transfers between devices: 8.48 us -> 5.53 us
  starting transfers between devices: 15.1 us -> 15.8 us
    ppermute x10 -> x7, waiting for transfers between devices: 8.48 us -> 1.77 us  [moved(): return lax.ppermute(block, ('seq', 'rate'), pairs)]
    ppermute x0 -> x3, starting transfers between devices: none -> 3.96 us  [traded(): lax.ppermute(block, 'seq', [(i, i ^ across * 2) for i in range(lax.axis_s...]
    ppermute x0 -> x3, waiting for transfers between devices: none -> 3.76 us  [traded(): lax.ppermute(block, 'seq', [(i, i ^ across * 2) for i in range(lax.axis_s...]
    ppermute x10 -> x7, starting transfers between devices: 15.1 us -> 11.8 us  [moved(): return lax.ppermute(block, ('seq', 'rate'), pairs)]
where the time goes in v2:
time: 29.3 us; the launch traced here: 28.9 us
  starting transfers between devices  15.8 us (54%)
  Pallas kernels  6.33 us (22%)
  waiting for transfers between devices  5.53 us (19%)
  between operations  1.3 us (4%)
    ppermute x7, starting transfers between devices, moved(): return lax.ppermute(block, ('seq', 'rate'), pairs)  11.8 us
    ppermute x3, starting transfers between devices, traded(): lax.ppermute(block, 'seq', [(i, i ^ across * 2) for i in range(lax.axis_s...  3.96 us
    ppermute x3, waiting for transfers between devices, traded(): lax.ppermute(block, 'seq', [(i, i ^ across * 2) for i in range(lax.axis_s...  3.76 us
    pallas_call x1, Pallas kernels, attend(): pl.pallas_call(main_kernel, out_shape=[jax.ShapeDtypeStruct((BLOCK, TOK),...  3.76 us
    ppermute x7, waiting for transfers between devices, moved(): return lax.ppermute(block, ('seq', 'rate'), pairs)  1.77 us
    pallas_call x1, Pallas kernels, prep(): pl.pallas_call(prep_kernel, out_shape=[jax.ShapeDtypeStruct((BLOCK + NOTE...  1.68 us
    pallas_call x1, Pallas kernels, final(): pl.pallas_call(final_kernel, out_shape=[jax.ShapeDtypeStruct((TOK, OWN),...  0.9 us
  transfers between devices with their start and end apart: 10, of which 7 were waited for; matrix products, arithmetic and copies ran while one was open for 0% of the time, Pallas kernels for 0%

profile of v2, /device:TPU:1, one launch (start us, length us, event | category | flops | bytes accessed | tf_op | source)
XLA Modules:
  0.0 28.9 jit_solution(7100098981498378807)
XLA Ops:
  1.3 1.7 %prep.1 = (bf16[400,128]{1,0:T(8,128)(2,1)S(1)}, bf16[400,128]{1,0:T(8,128)(2,1)S(1)}, bf16[384,128]{1,0:T(8,128)(2,1)S(1)}, bf16[384,128]{1,0:T(8,128)(2,1)S(1)}, bf16[400,128]{1,0:T(8,128)(2,1)S(1)}) custom-call(s32[1]{0:T(128)S(6)} %copy.5.bits, bf16[3,128,1536]{2,1,0:T(8,128)(2,1)} %bitcast.2, bf16[128,1536]{1,0:T(8,128)(2,1)} %cot.1), custom_call_target="tpu_custom_call" | custom-call | tf_op jit(solution)/shard_map/prep/pallas_call | solution.py:82
  3.0 4.7 %collective-permute-start = (bf16[400,128]{1,0:T(8,128)(2,1)S(1)}, bf16[400,128]{1,0:T(8,128)(2,1)S(1)}, u32[]{:S(2)}, u32[]{:S(2)}) collective-permute-start(bf16[400,128]{1,0:T(8,128)(2,1)S(1)} %get-tuple-element.14), channel_id=1, source_target_pairs={{0,9},{1,10},{2,11},{3,8},{4,14},{5,15},{6,12},{7,13},{8,17},{9,18... | collective-permute-start | bytes 307208 | tf_op jit(solution)/shard_map/ppermute | solution.py:279
  7.7 2.5 %collective-permute-start.1 = (bf16[384,128]{1,0:T(8,128)(2,1)S(1)}, bf16[384,128]{1,0:T(8,128)(2,1)S(1)}, u32[]{:S(2)}, u32[]{:S(2)}) collective-permute-start(bf16[384,128]{1,0:T(8,128)(2,1)S(1)} %get-tuple-element.15), channel_id=1, source_target_pairs={{0,16},{1,17},{2,18},{3,19},{4,20},{5,21},{6,22},{7,23},{8,24},{9,... | collective-permute-start | bytes 294920 | tf_op jit(solution)/shard_map/ppermute | solution.py:279
  10.2 1.1 %collective-permute-start.2 = (bf16[384,128]{1,0:T(8,128)(2,1)S(1)}, bf16[384,128]{1,0:T(8,128)(2,1)S(1)}, u32[]{:S(2)}, u32[]{:S(2)}) collective-permute-start(bf16[384,128]{1,0:T(8,128)(2,1)S(1)} %get-tuple-element.16), channel_id=1, source_target_pairs={{0,24},{1,25},{2,26},{3,27},{4,28},{5,29},{6,30},{7,31},{8,0},{9,1... | collective-permute-start | bytes 294920 | tf_op jit(solution)/shard_map/ppermute | solution.py:279
  11.3 1.2 %collective-permute-start.3 = (bf16[400,128]{1,0:T(8,128)(2,1)S(1)}, bf16[400,128]{1,0:T(8,128)(2,1)S(1)}, u32[]{:S(2)}, u32[]{:S(2)}) collective-permute-start(bf16[400,128]{1,0:T(8,128)(2,1)S(1)} %get-tuple-element.17), channel_id=1, source_target_pairs={{0,7},{1,4},{2,5},{3,6},{4,3},{5,0},{6,1},{7,2},{8,15},{9,12},{10,... | collective-permute-start | bytes 307208 | tf_op jit(solution)/shard_map/ppermute | solution.py:279
  12.5 0.0 collective-permute-done.rest_1_
  12.5 1.8 %collective-permute-start.4 = (bf16[400,128]{1,0:T(8,128)(2,1)S(1)}, bf16[400,128]{1,0:T(8,128)(2,1)S(1)}, u32[]{:S(2)}, u32[]{:S(2)}) collective-permute-start(bf16[400,128]{1,0:T(8,128)(2,1)S(1)} %collective-permute-done.rest_1_), channel_id=1, source_target_pairs={{0,4},{1,5},{2,6},{3,7},{4,0},{5,1},{6,2},{7,3},{8,12},{9,13},{10,... | collective-permute-start | bytes 307208 | tf_op jit(solution)/shard_map/ppermute | solution.py:279
  14.3 0.7 %collective-permute-done.1.rest_2_ = bf16[384,128]{1,0:T(8,128)(2,1)S(1)} collective-permute-done((bf16[384,128]{1,0:T(8,128)(2,1)S(1)}, bf16[384,128]{1,0:T(8,128)(2,1)S(1)}, u32[]{:S(2)}, u32[]{:S(2)}) %collective-permute-start.1) | collective-permute-done | bytes 98336 | tf_op jit(solution)/shard_map/ppermute | solution.py:279
  15.0 0.3 collective-permute-start.5
  15.2 0.0 collective-permute-done.2.rest_3_
  15.2 0.2 collective-permute-start.6
  15.5 0.2 collective-permute-done.3.rest_4_
  15.7 0.5 %collective-permute-done.5.rest_6_ = bf16[384,128]{1,0:T(8,128)(2,1)S(1)} collective-permute-done((bf16[384,128]{1,0:T(8,128)(2,1)S(1)}, bf16[384,128]{1,0:T(8,128)(2,1)S(1)}, u32[]{:S(2)}, u32[]{:S(2)}) %collective-permute-start.5) | collective-permute-done | bytes 98336 | tf_op jit(solution)/shard_map/ppermute | solution.py:279
  16.3 0.3 collective-permute-done.6.rest_7_
  16.5 0.0 collective-permute-done.4.rest_5_
  16.5 3.8 %attend.1 = (bf16[384,128]{1,0:T(8,128)(2,1)S(1)}, bf16[384,128]{1,0:T(8,128)(2,1)S(1)}, bf16[384,128]{1,0:T(8,128)(2,1)S(1)}, bf16[384,128]{1,0:T(8,128)(2,1)S(1)}) custom-call(bf16[400,128]{1,0:T(8,128)(2,1)S(1)} %get-tuple-element.13.rest_0_, bf16[400,128]{1,0:T(8,128)(2,1)S(1)} %collective-permute-done.rest_1_, ...), custom_call_target="tpu_custom_call" | custom-call | tf_op jit(solution)/shard_map/attend/pallas_call | solution.py:213
  20.3 2.5 %collective-permute-start.7 = (bf16[384,128]{1,0:T(8,128)(2,1)S(1)}, bf16[384,128]{1,0:T(8,128)(2,1)S(1)}, u32[]{:S(2)}, u32[]{:S(2)}) collective-permute-start(bf16[384,128]{1,0:T(8,128)(2,1)S(1)} %get-tuple-element.19), channel_id=1, source_target_pairs={{0,16},{4,20},{8,24},{12,28},{16,0},{20,4},{24,8},{28,12},{32,48},... | collective-permute-start | bytes 294920 | tf_op jit(solution)/shard_map/ppermute | solution.py:283
  22.8 1.5 %collective-permute-start.8 = (bf16[384,128]{1,0:T(8,128)(2,1)S(1)}, bf16[384,128]{1,0:T(8,128)(2,1)S(1)}, u32[]{:S(2)}, u32[]{:S(2)}) collective-permute-start(bf16[384,128]{1,0:T(8,128)(2,1)S(1)} %get-tuple-element.20), channel_id=1, source_target_pairs={{0,24},{4,28},{8,16},{12,20},{16,8},{20,12},{24,0},{28,4},{32,56},... | collective-permute-start | bytes 294920 | tf_op jit(solution)/shard_map/ppermute | solution.py:283
  24.3 0.0 collective-permute-start.9
  24.3 1.8 %collective-permute-done.7.rest_1_ = bf16[384,128]{1,0:T(8,128)(2,1)S(1)} collective-permute-done((bf16[384,128]{1,0:T(8,128)(2,1)S(1)}, bf16[384,128]{1,0:T(8,128)(2,1)S(1)}, u32[]{:S(2)}, u32[]{:S(2)}) %collective-permute-start.7) | collective-permute-done | bytes 98336 | tf_op jit(solution)/shard_map/ppermute | solution.py:283
  26.1 1.4 %collective-permute-done.8.rest_2_ = bf16[384,128]{1,0:T(8,128)(2,1)S(1)} collective-permute-done((bf16[384,128]{1,0:T(8,128)(2,1)S(1)}, bf16[384,128]{1,0:T(8,128)(2,1)S(1)}, u32[]{:S(2)}, u32[]{:S(2)}) %collective-permute-start.8) | collective-permute-done | bytes 98336 | tf_op jit(solution)/shard_map/ppermute | solution.py:283
  27.5 0.6 %collective-permute-done.9.rest_3_ = bf16[384,128]{1,0:T(8,128)(2,1)S(1)} collective-permute-done((bf16[384,128]{1,0:T(8,128)(2,1)S(1)}, bf16[384,128]{1,0:T(8,128)(2,1)S(1)}, u32[]{:S(2)}, u32[]{:S(2)}) %collective-permute-start.9) | collective-permute-done | bytes 98336 | tf_op jit(solution)/shard_map/ppermute | solution.py:283
  28.0 0.9 %final.1 = (bf16[128,384]{1,0:T(8,128)(2,1)}, bf16[3,128,384]{2,1,0:T(8,128)(2,1)}) custom-call(bf16[384,128]{1,0:T(8,128)(2,1)S(1)} %get-tuple-element.18.rest_0_, bf16[384,128]{1,0:T(8,128)(2,1)S(1)} %collective-permute-done.7.rest_1_, bf16[384,128]{1,0:T(8,128)(2,1)S(1)} %collective-permute-done.8.rest_2_, bf16[384,128]{1,0:T(8,128)(2,1)S(1)} %collective-permute-done.9.rest_3_), custom_call_target="tpu_custom_call" | custom-call | tf_op jit(solution)/shard_map/final/pallas_call | solution.py:261
Async XLA Ops:
  3.0 9.5 %collective-permute-start = (bf16[400,128]{1,0:T(8,128)(2,1)S(1)}, bf16[400,128]{1,0:T(8,128)(2,1)S(1)}, u32[]{:S(2)}, u32[]{:S(2)}) collective-permute-start(bf16[400,128]{1,0:T(8,128)(2,1)S(1)} %get-tuple-element.14), channel_id=1, source_target_pairs={{0,9},{1,10},{2,11},{3,8},{4,14},{5,15},{6,12},{7,13},{8,17},{9,18... | collective-permute-start | bytes 307208 | tf_op jit(solution)/shard_map/ppermute | solution.py:279
  7.7 7.2 %collective-permute-start.1 = (bf16[384,128]{1,0:T(8,128)(2,1)S(1)}, bf16[384,128]{1,0:T(8,128)(2,1)S(1)}, u32[]{:S(2)}, u32[]{:S(2)}) collective-permute-start(bf16[384,128]{1,0:T(8,128)(2,1)S(1)} %get-tuple-element.15), channel_id=1, source_target_pairs={{0,16},{1,17},{2,18},{3,19},{4,20},{5,21},{6,22},{7,23},{8,24},{9,... | collective-permute-start | bytes 294920 | tf_op jit(solution)/shard_map/ppermute | solution.py:279
  10.2 5.1 %collective-permute-start.2 = (bf16[384,128]{1,0:T(8,128)(2,1)S(1)}, bf16[384,128]{1,0:T(8,128)(2,1)S(1)}, u32[]{:S(2)}, u32[]{:S(2)}) collective-permute-start(bf16[384,128]{1,0:T(8,128)(2,1)S(1)} %get-tuple-element.16), channel_id=1, source_target_pairs={{0,24},{1,25},{2,26},{3,27},{4,28},{5,29},{6,30},{7,31},{8,0},{9,1... | collective-permute-start | bytes 294920 | tf_op jit(solution)/shard_map/ppermute | solution.py:279
  11.3 4.4 %collective-permute-start.3 = (bf16[400,128]{1,0:T(8,128)(2,1)S(1)}, bf16[400,128]{1,0:T(8,128)(2,1)S(1)}, u32[]{:S(2)}, u32[]{:S(2)}) collective-permute-start(bf16[400,128]{1,0:T(8,128)(2,1)S(1)} %get-tuple-element.17), channel_id=1, source_target_pairs={{0,7},{1,4},{2,5},{3,6},{4,3},{5,0},{6,1},{7,2},{8,15},{9,12},{10,... | collective-permute-start | bytes 307208 | tf_op jit(solution)/shard_map/ppermute | solution.py:279
  12.5 4.1 %collective-permute-start.4 = (bf16[400,128]{1,0:T(8,128)(2,1)S(1)}, bf16[400,128]{1,0:T(8,128)(2,1)S(1)}, u32[]{:S(2)}, u32[]{:S(2)}) collective-permute-start(bf16[400,128]{1,0:T(8,128)(2,1)S(1)} %collective-permute-done.rest_1_), channel_id=1, source_target_pairs={{0,4},{1,5},{2,6},{3,7},{4,0},{5,1},{6,2},{7,3},{8,12},{9,13},{10,... | collective-permute-start | bytes 307208 | tf_op jit(solution)/shard_map/ppermute | solution.py:279
  15.0 1.3 %collective-permute-start.5 = (bf16[384,128]{1,0:T(8,128)(2,1)S(1)}, bf16[384,128]{1,0:T(8,128)(2,1)S(1)}, u32[]{:S(2)}, u32[]{:S(2)}) collective-permute-start(bf16[384,128]{1,0:T(8,128)(2,1)S(1)} %collective-permute-done.1.rest_2_), channel_id=1, source_target_pairs={{0,4},{1,5},{2,6},{3,7},{4,0},{5,1},{6,2},{7,3},{8,12},{9,13},{10,... | collective-permute-start | bytes 294920 | tf_op jit(solution)/shard_map/ppermute | solution.py:279
  15.2 1.3 %collective-permute-start.6 = (bf16[384,128]{1,0:T(8,128)(2,1)S(1)}, bf16[384,128]{1,0:T(8,128)(2,1)S(1)}, u32[]{:S(2)}, u32[]{:S(2)}) collective-permute-start(bf16[384,128]{1,0:T(8,128)(2,1)S(1)} %collective-permute-done.2.rest_3_), channel_id=1, source_target_pairs={{0,4},{1,5},{2,6},{3,7},{4,0},{5,1},{6,2},{7,3},{8,12},{9,13},{10,... | collective-permute-start | bytes 294920 | tf_op jit(solution)/shard_map/ppermute | solution.py:279
  20.3 5.8 %collective-permute-start.7 = (bf16[384,128]{1,0:T(8,128)(2,1)S(1)}, bf16[384,128]{1,0:T(8,128)(2,1)S(1)}, u32[]{:S(2)}, u32[]{:S(2)}) collective-permute-start(bf16[384,128]{1,0:T(8,128)(2,1)S(1)} %get-tuple-element.19), channel_id=1, source_target_pairs={{0,16},{4,20},{8,24},{12,28},{16,0},{20,4},{24,8},{28,12},{32,48},... | collective-permute-start | bytes 294920 | tf_op jit(solution)/shard_map/ppermute | solution.py:283
  22.8 4.7 %collective-permute-start.8 = (bf16[384,128]{1,0:T(8,128)(2,1)S(1)}, bf16[384,128]{1,0:T(8,128)(2,1)S(1)}, u32[]{:S(2)}, u32[]{:S(2)}) collective-permute-start(bf16[384,128]{1,0:T(8,128)(2,1)S(1)} %get-tuple-element.20), channel_id=1, source_target_pairs={{0,24},{4,28},{8,16},{12,20},{16,8},{20,12},{24,0},{28,4},{32,56},... | collective-permute-start | bytes 294920 | tf_op jit(solution)/shard_map/ppermute | solution.py:283
  24.3 3.8 %collective-permute-start.9 = (bf16[384,128]{1,0:T(8,128)(2,1)S(1)}, bf16[384,128]{1,0:T(8,128)(2,1)S(1)}, u32[]{:S(2)}, u32[]{:S(2)}) collective-permute-start(bf16[384,128]{1,0:T(8,128)(2,1)S(1)} %get-tuple-element.21), channel_id=1, source_target_pairs={{0,8},{4,12},{8,0},{12,4},{16,24},{20,28},{24,16},{28,20},{32,40},... | collective-permute-start | bytes 294920 | tf_op jit(solution)/shard_map/ppermute | solution.py:283

commit v3 on v2

--- a/solution.py
+++ b/solution.py
@@ -142,7 +142,8 @@
     def products(c):
         cols = slice(c * WIDE, (c + 1) * WIDE)
         st[c] = lax.dot_general(ks[...], qs[cols], nt, preferred_element_type=F32)
-        dp[c] = lax.dot_general(vs[...], ds[cols], nt, preferred_element_type=F32)
+        keys = slice(0, SEG if c * WIDE < HALF else HALF)
+        dp[c, keys] = lax.dot_general(vs[keys], ds[cols], nt, preferred_element_type=F32)
 
     def weights(c):
         for i in range(c * WIDE // TOK, (c + 1) * WIDE // TOK):
@@ -187,10 +188,10 @@
             products(c + 1)
         weights(c)
         overs.append(scores(c))
+    gv[...] = lax.dot_general(et[:HALF], dn[...], nn, preferred_element_type=F32)
+    gk[...] = lax.dot_general(gt[:HALF], qn[...], nn, preferred_element_type=F32)
     part = lax.dot_general(ks[...], gt[:, :HALF], tn, preferred_element_type=F32)
     gq[...] = jnp.transpose(part * (jnp.concatenate(overs[: HALF // WIDE], axis=1) * SCALE))
-    gv[...] = lax.dot_general(et[:HALF], dn[...], nn, preferred_element_type=F32)
-    gk[...] = lax.dot_general(gt[:HALF], qn[...], nn, preferred_element_type=F32)
     made = []
     for d in range(4):
         rows = slice(d * TOK, (d + 1) * TOK)

time: 29.3 us -> 29.1 us (level)
  no operation moved by 1% of the time
where the time goes in v3:
time: 29.1 us; the launch traced here: 28.7 us
  starting transfers between devices  15.7 us (54%)
  Pallas kernels  6.13 us (21%)
  waiting for transfers between devices  5.53 us (19%)
  between operations  1.29 us (4%)
    ppermute x7, starting transfers between devices, moved(): return lax.ppermute(block, ('seq', 'rate'), pairs)  11.8 us
    ppermute x3, starting transfers between devices, traded(): lax.ppermute(block, 'seq', [(i, i ^ across * 2) for i in range(lax.axis_s...  3.93 us
    ppermute x3, waiting for transfers between devices, traded(): lax.ppermute(block, 'seq', [(i, i ^ across * 2) for i in range(lax.axis_s...  3.76 us
    pallas_call x1, Pallas kernels, attend(): pl.pallas_call(main_kernel, out_shape=[jax.ShapeDtypeStruct((BLOCK, TOK),...  3.56 us
    ppermute x7, waiting for transfers between devices, moved(): return lax.ppermute(block, ('seq', 'rate'), pairs)  1.77 us
    pallas_call x1, Pallas kernels, prep(): pl.pallas_call(prep_kernel, out_shape=[jax.ShapeDtypeStruct((BLOCK + NOTE...  1.68 us
    pallas_call x1, Pallas kernels, final(): pl.pallas_call(final_kernel, out_shape=[jax.ShapeDtypeStruct((TOK, OWN),...  0.9 us
  transfers between devices with their start and end apart: 10, of which 7 were waited for; matrix products, arithmetic and copies ran while one was open for 0% of the time, Pallas kernels for 0%

profile of v3, /device:TPU:1, one launch (start us, length us, event | category | flops | bytes accessed | tf_op | source)
XLA Modules:
  0.0 28.7 jit_solution(8690112565532898562)
XLA Ops:
  1.3 1.7 %prep.1 = (bf16[400,128]{1,0:T(8,128)(2,1)S(1)}, bf16[400,128]{1,0:T(8,128)(2,1)S(1)}, bf16[384,128]{1,0:T(8,128)(2,1)S(1)}, bf16[384,128]{1,0:T(8,128)(2,1)S(1)}, bf16[400,128]{1,0:T(8,128)(2,1)S(1)}) custom-call(s32[1]{0:T(128)S(6)} %copy.5.bits, bf16[3,128,1536]{2,1,0:T(8,128)(2,1)} %bitcast.2, bf16[128,1536]{1,0:T(8,128)(2,1)} %cot.1), custom_call_target="tpu_custom_call" | custom-call | tf_op jit(solution)/shard_map/prep/pallas_call | solution.py:82
  3.0 4.7 %collective-permute-start = (bf16[400,128]{1,0:T(8,128)(2,1)S(1)}, bf16[400,128]{1,0:T(8,128)(2,1)S(1)}, u32[]{:S(2)}, u32[]{:S(2)}) collective-permute-start(bf16[400,128]{1,0:T(8,128)(2,1)S(1)} %get-tuple-element.14), channel_id=1, source_target_pairs={{0,9},{1,10},{2,11},{3,8},{4,14},{5,15},{6,12},{7,13},{8,17},{9,18... | collective-permute-start | bytes 307208 | tf_op jit(solution)/shard_map/ppermute | solution.py:280
  7.7 2.5 %collective-permute-start.1 = (bf16[384,128]{1,0:T(8,128)(2,1)S(1)}, bf16[384,128]{1,0:T(8,128)(2,1)S(1)}, u32[]{:S(2)}, u32[]{:S(2)}) collective-permute-start(bf16[384,128]{1,0:T(8,128)(2,1)S(1)} %get-tuple-element.15), channel_id=1, source_target_pairs={{0,16},{1,17},{2,18},{3,19},{4,20},{5,21},{6,22},{7,23},{8,24},{9,... | collective-permute-start | bytes 294920 | tf_op jit(solution)/shard_map/ppermute | solution.py:280
  10.2 1.1 %collective-permute-start.2 = (bf16[384,128]{1,0:T(8,128)(2,1)S(1)}, bf16[384,128]{1,0:T(8,128)(2,1)S(1)}, u32[]{:S(2)}, u32[]{:S(2)}) collective-permute-start(bf16[384,128]{1,0:T(8,128)(2,1)S(1)} %get-tuple-element.16), channel_id=1, source_target_pairs={{0,24},{1,25},{2,26},{3,27},{4,28},{5,29},{6,30},{7,31},{8,0},{9,1... | collective-permute-start | bytes 294920 | tf_op jit(solution)/shard_map/ppermute | solution.py:280
  11.3 1.2 %collective-permute-start.3 = (bf16[400,128]{1,0:T(8,128)(2,1)S(1)}, bf16[400,128]{1,0:T(8,128)(2,1)S(1)}, u32[]{:S(2)}, u32[]{:S(2)}) collective-permute-start(bf16[400,128]{1,0:T(8,128)(2,1)S(1)} %get-tuple-element.17), channel_id=1, source_target_pairs={{0,7},{1,4},{2,5},{3,6},{4,3},{5,0},{6,1},{7,2},{8,15},{9,12},{10,... | collective-permute-start | bytes 307208 | tf_op jit(solution)/shard_map/ppermute | solution.py:280
  12.5 0.0 collective-permute-done.rest_1_
  12.5 1.8 %collective-permute-start.4 = (bf16[400,128]{1,0:T(8,128)(2,1)S(1)}, bf16[400,128]{1,0:T(8,128)(2,1)S(1)}, u32[]{:S(2)}, u32[]{:S(2)}) collective-permute-start(bf16[400,128]{1,0:T(8,128)(2,1)S(1)} %collective-permute-done.rest_1_), channel_id=1, source_target_pairs={{0,4},{1,5},{2,6},{3,7},{4,0},{5,1},{6,2},{7,3},{8,12},{9,13},{10,... | collective-permute-start | bytes 307208 | tf_op jit(solution)/shard_map/ppermute | solution.py:280
  14.3 0.7 %collective-permute-done.1.rest_2_ = bf16[384,128]{1,0:T(8,128)(2,1)S(1)} collective-permute-done((bf16[384,128]{1,0:T(8,128)(2,1)S(1)}, bf16[384,128]{1,0:T(8,128)(2,1)S(1)}, u32[]{:S(2)}, u32[]{:S(2)}) %collective-permute-start.1) | collective-permute-done | bytes 98336 | tf_op jit(solution)/shard_map/ppermute | solution.py:280
  15.0 0.3 collective-permute-start.5
  15.2 0.0 collective-permute-done.2.rest_3_
  15.2 0.2 collective-permute-start.6
  15.5 0.2 collective-permute-done.3.rest_4_
  15.7 0.5 %collective-permute-done.5.rest_6_ = bf16[384,128]{1,0:T(8,128)(2,1)S(1)} collective-permute-done((bf16[384,128]{1,0:T(8,128)(2,1)S(1)}, bf16[384,128]{1,0:T(8,128)(2,1)S(1)}, u32[]{:S(2)}, u32[]{:S(2)}) %collective-permute-start.5) | collective-permute-done | bytes 98336 | tf_op jit(solution)/shard_map/ppermute | solution.py:280
  16.3 0.3 %collective-permute-done.6.rest_7_ = bf16[384,128]{1,0:T(8,128)(2,1)S(1)} collective-permute-done((bf16[384,128]{1,0:T(8,128)(2,1)S(1)}, bf16[384,128]{1,0:T(8,128)(2,1)S(1)}, u32[]{:S(2)}, u32[]{:S(2)}) %collective-permute-start.6) | collective-permute-done | bytes 98336 | tf_op jit(solution)/shard_map/ppermute | solution.py:280
  16.5 0.0 collective-permute-done.4.rest_5_
  16.5 3.6 %attend.1 = (bf16[384,128]{1,0:T(8,128)(2,1)S(1)}, bf16[384,128]{1,0:T(8,128)(2,1)S(1)}, bf16[384,128]{1,0:T(8,128)(2,1)S(1)}, bf16[384,128]{1,0:T(8,128)(2,1)S(1)}) custom-call(bf16[400,128]{1,0:T(8,128)(2,1)S(1)} %get-tuple-element.13.rest_0_, bf16[400,128]{1,0:T(8,128)(2,1)S(1)} %collective-permute-done.rest_1_, ...), custom_call_target="tpu_custom_call" | custom-call | tf_op jit(solution)/shard_map/attend/pallas_call | solution.py:214
  20.1 2.5 %collective-permute-start.7 = (bf16[384,128]{1,0:T(8,128)(2,1)S(1)}, bf16[384,128]{1,0:T(8,128)(2,1)S(1)}, u32[]{:S(2)}, u32[]{:S(2)}) collective-permute-start(bf16[384,128]{1,0:T(8,128)(2,1)S(1)} %get-tuple-element.19), channel_id=1, source_target_pairs={{0,16},{4,20},{8,24},{12,28},{16,0},{20,4},{24,8},{28,12},{32,48},... | collective-permute-start | bytes 294920 | tf_op jit(solution)/shard_map/ppermute | solution.py:284
  22.6 1.5 %collective-permute-start.8 = (bf16[384,128]{1,0:T(8,128)(2,1)S(1)}, bf16[384,128]{1,0:T(8,128)(2,1)S(1)}, u32[]{:S(2)}, u32[]{:S(2)}) collective-permute-start(bf16[384,128]{1,0:T(8,128)(2,1)S(1)} %get-tuple-element.20), channel_id=1, source_target_pairs={{0,24},{4,28},{8,16},{12,20},{16,8},{20,12},{24,0},{28,4},{32,56},... | collective-permute-start | bytes 294920 | tf_op jit(solution)/shard_map/ppermute | solution.py:284
  24.0 0.0 collective-permute-start.9
  24.0 1.8 %collective-permute-done.7.rest_1_ = bf16[384,128]{1,0:T(8,128)(2,1)S(1)} collective-permute-done((bf16[384,128]{1,0:T(8,128)(2,1)S(1)}, bf16[384,128]{1,0:T(8,128)(2,1)S(1)}, u32[]{:S(2)}, u32[]{:S(2)}) %collective-permute-start.7) | collective-permute-done | bytes 98336 | tf_op jit(solution)/shard_map/ppermute | solution.py:284
  25.9 1.4 %collective-permute-done.8.rest_2_ = bf16[384,128]{1,0:T(8,128)(2,1)S(1)} collective-permute-done((bf16[384,128]{1,0:T(8,128)(2,1)S(1)}, bf16[384,128]{1,0:T(8,128)(2,1)S(1)}, u32[]{:S(2)}, u32[]{:S(2)}) %collective-permute-start.8) | collective-permute-done | bytes 98336 | tf_op jit(solution)/shard_map/ppermute | solution.py:284
  27.3 0.5 %collective-permute-done.9.rest_3_ = bf16[384,128]{1,0:T(8,128)(2,1)S(1)} collective-permute-done((bf16[384,128]{1,0:T(8,128)(2,1)S(1)}, bf16[384,128]{1,0:T(8,128)(2,1)S(1)}, u32[]{:S(2)}, u32[]{:S(2)}) %collective-permute-start.9) | collective-permute-done | bytes 98336 | tf_op jit(solution)/shard_map/ppermute | solution.py:284
  27.8 0.9 %final.1 = (bf16[128,384]{1,0:T(8,128)(2,1)}, bf16[3,128,384]{2,1,0:T(8,128)(2,1)}) custom-call(bf16[384,128]{1,0:T(8,128)(2,1)S(1)} %get-tuple-element.18.rest_0_, bf16[384,128]{1,0:T(8,128)(2,1)S(1)} %collective-permute-done.7.rest_1_, bf16[384,128]{1,0:T(8,128)(2,1)S(1)} %collective-permute-done.8.rest_2_, bf16[384,128]{1,0:T(8,128)(2,1)S(1)} %collective-permute-done.9.rest_3_), custom_call_target="tpu_custom_call" | custom-call | tf_op jit(solution)/shard_map/final/pallas_call | solution.py:262
Async XLA Ops:
  3.0 9.5 %collective-permute-start = (bf16[400,128]{1,0:T(8,128)(2,1)S(1)}, bf16[400,128]{1,0:T(8,128)(2,1)S(1)}, u32[]{:S(2)}, u32[]{:S(2)}) collective-permute-start(bf16[400,128]{1,0:T(8,128)(2,1)S(1)} %get-tuple-element.14), channel_id=1, source_target_pairs={{0,9},{1,10},{2,11},{3,8},{4,14},{5,15},{6,12},{7,13},{8,17},{9,18... | collective-permute-start | bytes 307208 | tf_op jit(solution)/shard_map/ppermute | solution.py:280
  7.7 7.2 %collective-permute-start.1 = (bf16[384,128]{1,0:T(8,128)(2,1)S(1)}, bf16[384,128]{1,0:T(8,128)(2,1)S(1)}, u32[]{:S(2)}, u32[]{:S(2)}) collective-permute-start(bf16[384,128]{1,0:T(8,128)(2,1)S(1)} %get-tuple-element.15), channel_id=1, source_target_pairs={{0,16},{1,17},{2,18},{3,19},{4,20},{5,21},{6,22},{7,23},{8,24},{9,... | collective-permute-start | bytes 294920 | tf_op jit(solution)/shard_map/ppermute | solution.py:280
  10.2 5.1 %collective-permute-start.2 = (bf16[384,128]{1,0:T(8,128)(2,1)S(1)}, bf16[384,128]{1,0:T(8,128)(2,1)S(1)}, u32[]{:S(2)}, u32[]{:S(2)}) collective-permute-start(bf16[384,128]{1,0:T(8,128)(2,1)S(1)} %get-tuple-element.16), channel_id=1, source_target_pairs={{0,24},{1,25},{2,26},{3,27},{4,28},{5,29},{6,30},{7,31},{8,0},{9,1... | collective-permute-start | bytes 294920 | tf_op jit(solution)/shard_map/ppermute | solution.py:280
  11.3 4.4 %collective-permute-start.3 = (bf16[400,128]{1,0:T(8,128)(2,1)S(1)}, bf16[400,128]{1,0:T(8,128)(2,1)S(1)}, u32[]{:S(2)}, u32[]{:S(2)}) collective-permute-start(bf16[400,128]{1,0:T(8,128)(2,1)S(1)} %get-tuple-element.17), channel_id=1, source_target_pairs={{0,7},{1,4},{2,5},{3,6},{4,3},{5,0},{6,1},{7,2},{8,15},{9,12},{10,... | collective-permute-start | bytes 307208 | tf_op jit(solution)/shard_map/ppermute | solution.py:280
  12.5 4.1 %collective-permute-start.4 = (bf16[400,128]{1,0:T(8,128)(2,1)S(1)}, bf16[400,128]{1,0:T(8,128)(2,1)S(1)}, u32[]{:S(2)}, u32[]{:S(2)}) collective-permute-start(bf16[400,128]{1,0:T(8,128)(2,1)S(1)} %collective-permute-done.rest_1_), channel_id=1, source_target_pairs={{0,4},{1,5},{2,6},{3,7},{4,0},{5,1},{6,2},{7,3},{8,12},{9,13},{10,... | collective-permute-start | bytes 307208 | tf_op jit(solution)/shard_map/ppermute | solution.py:280
  15.0 1.3 %collective-permute-start.5 = (bf16[384,128]{1,0:T(8,128)(2,1)S(1)}, bf16[384,128]{1,0:T(8,128)(2,1)S(1)}, u32[]{:S(2)}, u32[]{:S(2)}) collective-permute-start(bf16[384,128]{1,0:T(8,128)(2,1)S(1)} %collective-permute-done.1.rest_2_), channel_id=1, source_target_pairs={{0,4},{1,5},{2,6},{3,7},{4,0},{5,1},{6,2},{7,3},{8,12},{9,13},{10,... | collective-permute-start | bytes 294920 | tf_op jit(solution)/shard_map/ppermute | solution.py:280
  15.2 1.3 %collective-permute-start.6 = (bf16[384,128]{1,0:T(8,128)(2,1)S(1)}, bf16[384,128]{1,0:T(8,128)(2,1)S(1)}, u32[]{:S(2)}, u32[]{:S(2)}) collective-permute-start(bf16[384,128]{1,0:T(8,128)(2,1)S(1)} %collective-permute-done.2.rest_3_), channel_id=1, source_target_pairs={{0,4},{1,5},{2,6},{3,7},{4,0},{5,1},{6,2},{7,3},{8,12},{9,13},{10,... | collective-permute-start | bytes 294920 | tf_op jit(solution)/shard_map/ppermute | solution.py:280
  20.1 5.7 %collective-permute-start.7 = (bf16[384,128]{1,0:T(8,128)(2,1)S(1)}, bf16[384,128]{1,0:T(8,128)(2,1)S(1)}, u32[]{:S(2)}, u32[]{:S(2)}) collective-permute-start(bf16[384,128]{1,0:T(8,128)(2,1)S(1)} %get-tuple-element.19), channel_id=1, source_target_pairs={{0,16},{4,20},{8,24},{12,28},{16,0},{20,4},{24,8},{28,12},{32,48},... | collective-permute-start | bytes 294920 | tf_op jit(solution)/shard_map/ppermute | solution.py:284
  22.6 4.7 %collective-permute-start.8 = (bf16[384,128]{1,0:T(8,128)(2,1)S(1)}, bf16[384,128]{1,0:T(8,128)(2,1)S(1)}, u32[]{:S(2)}, u32[]{:S(2)}) collective-permute-start(bf16[384,128]{1,0:T(8,128)(2,1)S(1)} %get-tuple-element.20), channel_id=1, source_target_pairs={{0,24},{4,28},{8,16},{12,20},{16,8},{20,12},{24,0},{28,4},{32,56},... | collective-permute-start | bytes 294920 | tf_op jit(solution)/shard_map/ppermute | solution.py:284
  24.0 3.8 %collective-permute-start.9 = (bf16[384,128]{1,0:T(8,128)(2,1)S(1)}, bf16[384,128]{1,0:T(8,128)(2,1)S(1)}, u32[]{:S(2)}, u32[]{:S(2)}) collective-permute-start(bf16[384,128]{1,0:T(8,128)(2,1)S(1)} %get-tuple-element.21), channel_id=1, source_target_pairs={{0,8},{4,12},{8,0},{12,4},{16,24},{20,28},{24,16},{28,20},{32,40},... | collective-permute-start | bytes 294920 | tf_op jit(solution)/shard_map/ppermute | solution.py:284

commit v4 on v3

--- a/solution.py
+++ b/solution.py
@@ -21,6 +21,7 @@
 F32 = jnp.float32
 MADE = ((0, (0, 0), True), (1, (1, 2), True), (2, (0, 0), False), (3, (0, 0), False), (0, (3, 3), True))
 BACK = (0, 2, 3, 1)
+AHEAD = (0, 2, 1, 3)
 BLOCK = 3 * TOK
 NOTE = 16
 WIDE = 256
@@ -107,7 +108,7 @@
 
 
 def main_kernel(*rest):
-    ins = rest[:8]
+    ins = [rest[AHEAD.index(s % 4) + s // 4 * 4] for s in range(8)]
     outs = rest[8:12]
     qs, ks, vs, ds, bias, st, dp, et, gt, qn, dn, out, gq, gk, gv = rest[12:]
     odd = chip_index() & 1
@@ -288,7 +289,7 @@
     sent = prep(dilation_bits, jnp.transpose(projections, (1, 0, 2)), grad_out)
     near = [sent[0]] + [moved(sent[e], MADE[e][0], 0, MADE[e][1]) for e in range(1, CHIPS)]
     far = [moved(sent[CHIPS], 0, 1, MADE[CHIPS][1])] + [moved(block, 0, 1, (0, 0)) for block in near[1:]]
-    results = attend(near + far)
+    results = attend([near[d] for d in AHEAD] + [far[d] for d in AHEAD])
     back = [traded(results[k], k) if k else results[k] for k in BACK]
     attended, grads = final(back)
     return attended, jnp.transpose(grads, (1, 0, 2))

time: 29.1 us -> 29.1 us (level)
  no operation moved by 1% of the time
where the time goes in v4:
time: 29.1 us; the launch traced here: 28.7 us
  starting transfers between devices  15.7 us (54%)
  Pallas kernels  6.13 us (21%)
  waiting for transfers between devices  5.53 us (19%)
  between operations  1.29 us (4%)
    ppermute x7, starting transfers between devices, moved(): return lax.ppermute(block, ('seq', 'rate'), pairs)  11.8 us
    ppermute x3, starting transfers between devices, traded(): lax.ppermute(block, 'seq', [(i, i ^ across * 2) for i in range(lax.axis_s...  3.94 us
    ppermute x3, waiting for transfers between devices, traded(): lax.ppermute(block, 'seq', [(i, i ^ across * 2) for i in range(lax.axis_s...  3.76 us
    pallas_call x1, Pallas kernels, attend(): pl.pallas_call(main_kernel, out_shape=[jax.ShapeDtypeStruct((BLOCK, TOK),...  3.56 us
    ppermute x7, waiting for transfers between devices, moved(): return lax.ppermute(block, ('seq', 'rate'), pairs)  1.77 us
    pallas_call x1, Pallas kernels, prep(): pl.pallas_call(prep_kernel, out_shape=[jax.ShapeDtypeStruct((BLOCK + NOTE...  1.68 us
    pallas_call x1, Pallas kernels, final(): pl.pallas_call(final_kernel, out_shape=[jax.ShapeDtypeStruct((TOK, OWN),...  0.9 us
  transfers between devices with their start and end apart: 10, of which 7 were waited for; matrix products, arithmetic and copies ran while one was open for 0% of the time, Pallas kernels for 0%

profile of v4, /device:TPU:1, one launch (start us, length us, event | category | flops | bytes accessed | tf_op | source)
XLA Modules:
  0.0 28.7 jit_solution(11689359504841119609)
XLA Ops:
  1.3 1.7 %prep.1 = (bf16[400,128]{1,0:T(8,128)(2,1)S(1)}, bf16[400,128]{1,0:T(8,128)(2,1)S(1)}, bf16[384,128]{1,0:T(8,128)(2,1)S(1)}, bf16[384,128]{1,0:T(8,128)(2,1)S(1)}, bf16[400,128]{1,0:T(8,128)(2,1)S(1)}) custom-call(s32[1]{0:T(128)S(6)} %copy.5.bits, bf16[3,128,1536]{2,1,0:T(8,128)(2,1)} %bitcast.2, bf16[128,1536]{1,0:T(8,128)(2,1)} %cot.1), custom_call_target="tpu_custom_call" | custom-call | tf_op jit(solution)/shard_map/prep/pallas_call | solution.py:83
  3.0 4.7 %collective-permute-start.1 = (bf16[400,128]{1,0:T(8,128)(2,1)S(1)}, bf16[400,128]{1,0:T(8,128)(2,1)S(1)}, u32[]{:S(2)}, u32[]{:S(2)}) collective-permute-start(bf16[400,128]{1,0:T(8,128)(2,1)S(1)} %get-tuple-element.15), channel_id=1, source_target_pairs={{0,9},{1,10},{2,11},{3,8},{4,14},{5,15},{6,12},{7,13},{8,17},{9,18... | collective-permute-start | bytes 307208 | tf_op jit(solution)/shard_map/ppermute | solution.py:281
  7.7 2.5 %collective-permute-start = (bf16[384,128]{1,0:T(8,128)(2,1)S(1)}, bf16[384,128]{1,0:T(8,128)(2,1)S(1)}, u32[]{:S(2)}, u32[]{:S(2)}) collective-permute-start(bf16[384,128]{1,0:T(8,128)(2,1)S(1)} %get-tuple-element.14), channel_id=1, source_target_pairs={{0,16},{1,17},{2,18},{3,19},{4,20},{5,21},{6,22},{7,23},{8,24},{9,... | collective-permute-start | bytes 294920 | tf_op jit(solution)/shard_map/ppermute | solution.py:281
  10.2 1.1 %collective-permute-start.2 = (bf16[384,128]{1,0:T(8,128)(2,1)S(1)}, bf16[384,128]{1,0:T(8,128)(2,1)S(1)}, u32[]{:S(2)}, u32[]{:S(2)}) collective-permute-start(bf16[384,128]{1,0:T(8,128)(2,1)S(1)} %get-tuple-element.16), channel_id=1, source_target_pairs={{0,24},{1,25},{2,26},{3,27},{4,28},{5,29},{6,30},{7,31},{8,0},{9,1... | collective-permute-start | bytes 294920 | tf_op jit(solution)/shard_map/ppermute | solution.py:281
  11.3 1.2 %collective-permute-start.3 = (bf16[400,128]{1,0:T(8,128)(2,1)S(1)}, bf16[400,128]{1,0:T(8,128)(2,1)S(1)}, u32[]{:S(2)}, u32[]{:S(2)}) collective-permute-start(bf16[400,128]{1,0:T(8,128)(2,1)S(1)} %get-tuple-element.17), channel_id=1, source_target_pairs={{0,7},{1,4},{2,5},{3,6},{4,3},{5,0},{6,1},{7,2},{8,15},{9,12},{10,... | collective-permute-start | bytes 307208 | tf_op jit(solution)/shard_map/ppermute | solution.py:281
  12.5 0.0 collective-permute-done.1.rest_2_
  12.5 1.8 %collective-permute-start.5 = (bf16[400,128]{1,0:T(8,128)(2,1)S(1)}, bf16[400,128]{1,0:T(8,128)(2,1)S(1)}, u32[]{:S(2)}, u32[]{:S(2)}) collective-permute-start(bf16[400,128]{1,0:T(8,128)(2,1)S(1)} %collective-permute-done.1.rest_2_), channel_id=1, source_target_pairs={{0,4},{1,5},{2,6},{3,7},{4,0},{5,1},{6,2},{7,3},{8,12},{9,13},{10,... | collective-permute-start | bytes 307208 | tf_op jit(solution)/shard_map/ppermute | solution.py:281
  14.3 0.7 %collective-permute-done.rest_1_ = bf16[384,128]{1,0:T(8,128)(2,1)S(1)} collective-permute-done((bf16[384,128]{1,0:T(8,128)(2,1)S(1)}, bf16[384,128]{1,0:T(8,128)(2,1)S(1)}, u32[]{:S(2)}, u32[]{:S(2)}) %collective-permute-start) | collective-permute-done | bytes 98336 | tf_op jit(solution)/shard_map/ppermute | solution.py:281
  15.0 0.3 collective-permute-start.4
  15.2 0.0 collective-permute-done.2.rest_3_
  15.2 0.2 collective-permute-start.6
  15.5 0.2 collective-permute-done.3.rest_4_
  15.7 0.5 %collective-permute-done.4.rest_5_ = bf16[384,128]{1,0:T(8,128)(2,1)S(1)} collective-permute-done((bf16[384,128]{1,0:T(8,128)(2,1)S(1)}, bf16[384,128]{1,0:T(8,128)(2,1)S(1)}, u32[]{:S(2)}, u32[]{:S(2)}) %collective-permute-start.4) | collective-permute-done | bytes 98336 | tf_op jit(solution)/shard_map/ppermute | solution.py:281
  16.3 0.3 %collective-permute-done.6.rest_7_ = bf16[384,128]{1,0:T(8,128)(2,1)S(1)} collective-permute-done((bf16[384,128]{1,0:T(8,128)(2,1)S(1)}, bf16[384,128]{1,0:T(8,128)(2,1)S(1)}, u32[]{:S(2)}, u32[]{:S(2)}) %collective-permute-start.6) | collective-permute-done | bytes 98336 | tf_op jit(solution)/shard_map/ppermute | solution.py:281
  16.5 0.0 collective-permute-done.5.rest_6_
  16.5 3.6 %attend.1 = (bf16[384,128]{1,0:T(8,128)(2,1)S(1)}, bf16[384,128]{1,0:T(8,128)(2,1)S(1)}, bf16[384,128]{1,0:T(8,128)(2,1)S(1)}, bf16[384,128]{1,0:T(8,128)(2,1)S(1)}) custom-call(bf16[400,128]{1,0:T(8,128)(2,1)S(1)} %get-tuple-element.13.rest_0_, bf16[384,128]{1,0:T(8,128)(2,1)S(1)} %collective-permute-done.rest_1_, ...), custom_call_target="tpu_custom_call" | custom-call | tf_op jit(solution)/shard_map/attend/pallas_call | solution.py:215
  20.1 2.5 %collective-permute-start.7 = (bf16[384,128]{1,0:T(8,128)(2,1)S(1)}, bf16[384,128]{1,0:T(8,128)(2,1)S(1)}, u32[]{:S(2)}, u32[]{:S(2)}) collective-permute-start(bf16[384,128]{1,0:T(8,128)(2,1)S(1)} %get-tuple-element.19), channel_id=1, source_target_pairs={{0,16},{4,20},{8,24},{12,28},{16,0},{20,4},{24,8},{28,12},{32,48},... | collective-permute-start | bytes 294920 | tf_op jit(solution)/shard_map/ppermute | solution.py:285
  22.6 1.5 %collective-permute-start.8 = (bf16[384,128]{1,0:T(8,128)(2,1)S(1)}, bf16[384,128]{1,0:T(8,128)(2,1)S(1)}, u32[]{:S(2)}, u32[]{:S(2)}) collective-permute-start(bf16[384,128]{1,0:T(8,128)(2,1)S(1)} %get-tuple-element.20), channel_id=1, source_target_pairs={{0,24},{4,28},{8,16},{12,20},{16,8},{20,12},{24,0},{28,4},{32,56},... | collective-permute-start | bytes 294920 | tf_op jit(solution)/shard_map/ppermute | solution.py:285
  24.0 0.0 collective-permute-start.9
  24.0 1.8 %collective-permute-done.7.rest_1_ = bf16[384,128]{1,0:T(8,128)(2,1)S(1)} collective-permute-done((bf16[384,128]{1,0:T(8,128)(2,1)S(1)}, bf16[384,128]{1,0:T(8,128)(2,1)S(1)}, u32[]{:S(2)}, u32[]{:S(2)}) %collective-permute-start.7) | collective-permute-done | bytes 98336 | tf_op jit(solution)/shard_map/ppermute | solution.py:285
  25.9 1.4 %collective-permute-done.8.rest_2_ = bf16[384,128]{1,0:T(8,128)(2,1)S(1)} collective-permute-done((bf16[384,128]{1,0:T(8,128)(2,1)S(1)}, bf16[384,128]{1,0:T(8,128)(2,1)S(1)}, u32[]{:S(2)}, u32[]{:S(2)}) %collective-permute-start.8) | collective-permute-done | bytes 98336 | tf_op jit(solution)/shard_map/ppermute | solution.py:285
  27.3 0.5 %collective-permute-done.9.rest_3_ = bf16[384,128]{1,0:T(8,128)(2,1)S(1)} collective-permute-done((bf16[384,128]{1,0:T(8,128)(2,1)S(1)}, bf16[384,128]{1,0:T(8,128)(2,1)S(1)}, u32[]{:S(2)}, u32[]{:S(2)}) %collective-permute-start.9) | collective-permute-done | bytes 98336 | tf_op jit(solution)/shard_map/ppermute | solution.py:285
  27.8 0.9 %final.1 = (bf16[128,384]{1,0:T(8,128)(2,1)}, bf16[3,128,384]{2,1,0:T(8,128)(2,1)}) custom-call(bf16[384,128]{1,0:T(8,128)(2,1)S(1)} %get-tuple-element.18.rest_0_, bf16[384,128]{1,0:T(8,128)(2,1)S(1)} %collective-permute-done.7.rest_1_, bf16[384,128]{1,0:T(8,128)(2,1)S(1)} %collective-permute-done.8.rest_2_, bf16[384,128]{1,0:T(8,128)(2,1)S(1)} %collective-permute-done.9.rest_3_), custom_call_target="tpu_custom_call" | custom-call | tf_op jit(solution)/shard_map/final/pallas_call | solution.py:263
Async XLA Ops:
  3.0 9.5 %collective-permute-start.1 = (bf16[400,128]{1,0:T(8,128)(2,1)S(1)}, bf16[400,128]{1,0:T(8,128)(2,1)S(1)}, u32[]{:S(2)}, u32[]{:S(2)}) collective-permute-start(bf16[400,128]{1,0:T(8,128)(2,1)S(1)} %get-tuple-element.15), channel_id=1, source_target_pairs={{0,9},{1,10},{2,11},{3,8},{4,14},{5,15},{6,12},{7,13},{8,17},{9,18... | collective-permute-start | bytes 307208 | tf_op jit(solution)/shard_map/ppermute | solution.py:281
  7.7 7.2 %collective-permute-start = (bf16[384,128]{1,0:T(8,128)(2,1)S(1)}, bf16[384,128]{1,0:T(8,128)(2,1)S(1)}, u32[]{:S(2)}, u32[]{:S(2)}) collective-permute-start(bf16[384,128]{1,0:T(8,128)(2,1)S(1)} %get-tuple-element.14), channel_id=1, source_target_pairs={{0,16},{1,17},{2,18},{3,19},{4,20},{5,21},{6,22},{7,23},{8,24},{9,... | collective-permute-start | bytes 294920 | tf_op jit(solution)/shard_map/ppermute | solution.py:281
  10.2 5.1 %collective-permute-start.2 = (bf16[384,128]{1,0:T(8,128)(2,1)S(1)}, bf16[384,128]{1,0:T(8,128)(2,1)S(1)}, u32[]{:S(2)}, u32[]{:S(2)}) collective-permute-start(bf16[384,128]{1,0:T(8,128)(2,1)S(1)} %get-tuple-element.16), channel_id=1, source_target_pairs={{0,24},{1,25},{2,26},{3,27},{4,28},{5,29},{6,30},{7,31},{8,0},{9,1... | collective-permute-start | bytes 294920 | tf_op jit(solution)/shard_map/ppermute | solution.py:281
  11.3 4.4 %collective-permute-start.3 = (bf16[400,128]{1,0:T(8,128)(2,1)S(1)}, bf16[400,128]{1,0:T(8,128)(2,1)S(1)}, u32[]{:S(2)}, u32[]{:S(2)}) collective-permute-start(bf16[400,128]{1,0:T(8,128)(2,1)S(1)} %get-tuple-element.17), channel_id=1, source_target_pairs={{0,7},{1,4},{2,5},{3,6},{4,3},{5,0},{6,1},{7,2},{8,15},{9,12},{10,... | collective-permute-start | bytes 307208 | tf_op jit(solution)/shard_map/ppermute | solution.py:281
  12.5 4.1 %collective-permute-start.5 = (bf16[400,128]{1,0:T(8,128)(2,1)S(1)}, bf16[400,128]{1,0:T(8,128)(2,1)S(1)}, u32[]{:S(2)}, u32[]{:S(2)}) collective-permute-start(bf16[400,128]{1,0:T(8,128)(2,1)S(1)} %collective-permute-done.1.rest_2_), channel_id=1, source_target_pairs={{0,4},{1,5},{2,6},{3,7},{4,0},{5,1},{6,2},{7,3},{8,12},{9,13},{10,... | collective-permute-start | bytes 307208 | tf_op jit(solution)/shard_map/ppermute | solution.py:281
  15.0 1.3 %collective-permute-start.4 = (bf16[384,128]{1,0:T(8,128)(2,1)S(1)}, bf16[384,128]{1,0:T(8,128)(2,1)S(1)}, u32[]{:S(2)}, u32[]{:S(2)}) collective-permute-start(bf16[384,128]{1,0:T(8,128)(2,1)S(1)} %collective-permute-done.rest_1_), channel_id=1, source_target_pairs={{0,4},{1,5},{2,6},{3,7},{4,0},{5,1},{6,2},{7,3},{8,12},{9,13},{10,... | collective-permute-start | bytes 294920 | tf_op jit(solution)/shard_map/ppermute | solution.py:281
  15.2 1.3 %collective-permute-start.6 = (bf16[384,128]{1,0:T(8,128)(2,1)S(1)}, bf16[384,128]{1,0:T(8,128)(2,1)S(1)}, u32[]{:S(2)}, u32[]{:S(2)}) collective-permute-start(bf16[384,128]{1,0:T(8,128)(2,1)S(1)} %collective-permute-done.2.rest_3_), channel_id=1, source_target_pairs={{0,4},{1,5},{2,6},{3,7},{4,0},{5,1},{6,2},{7,3},{8,12},{9,13},{10,... | collective-permute-start | bytes 294920 | tf_op jit(solution)/shard_map/ppermute | solution.py:281
  20.1 5.8 %collective-permute-start.7 = (bf16[384,128]{1,0:T(8,128)(2,1)S(1)}, bf16[384,128]{1,0:T(8,128)(2,1)S(1)}, u32[]{:S(2)}, u32[]{:S(2)}) collective-permute-start(bf16[384,128]{1,0:T(8,128)(2,1)S(1)} %get-tuple-element.19), channel_id=1, source_target_pairs={{0,16},{4,20},{8,24},{12,28},{16,0},{20,4},{24,8},{28,12},{32,48},... | collective-permute-start | bytes 294920 | tf_op jit(solution)/shard_map/ppermute | solution.py:285
  22.6 4.7 %collective-permute-start.8 = (bf16[384,128]{1,0:T(8,128)(2,1)S(1)}, bf16[384,128]{1,0:T(8,128)(2,1)S(1)}, u32[]{:S(2)}, u32[]{:S(2)}) collective-permute-start(bf16[384,128]{1,0:T(8,128)(2,1)S(1)} %get-tuple-element.20), channel_id=1, source_target_pairs={{0,24},{4,28},{8,16},{12,20},{16,8},{20,12},{24,0},{28,4},{32,56},... | collective-permute-start | bytes 294920 | tf_op jit(solution)/shard_map/ppermute | solution.py:285
  24.0 3.8 %collective-permute-start.9 = (bf16[384,128]{1,0:T(8,128)(2,1)S(1)}, bf16[384,128]{1,0:T(8,128)(2,1)S(1)}, u32[]{:S(2)}, u32[]{:S(2)}) collective-permute-start(bf16[384,128]{1,0:T(8,128)(2,1)S(1)} %get-tuple-element.21), channel_id=1, source_target_pairs={{0,8},{4,12},{8,0},{12,4},{16,24},{20,28},{24,16},{28,20},{32,40},... | collective-permute-start | bytes 294920 | tf_op jit(solution)/shard_map/ppermute | solution.py:285
